TPU v7x, 32 devices: a whole 2x2x4 slice. The times are simulated.
32 devices in a mesh: rad: 8 (over y, x, core), az: 4 (over z).
Axes of the slice: x: 2, y: 2, z: 4, core: 2. Of those that a mesh axis runs over, the one named last changes fastest.
Arguments:
- fields: float32 [5, 48, 8, 1024], P(None, 'rad', None, 'az'), may hold values from -0.9 to 4, as said below
- shifts: int32 [48], P('rad'), may hold values from 0 to 768, as said below
Outputs:
- advanced: float32 [5, 48, 8, 1024], P(None, 'rad', None, 'az')
Inputs may be any that keep to these rules, and one draw needn't show every extreme that they name: `fields`: components 0 (density) and 4 (pressure) lie in 2.0 to 4.0; components 1 to 3 (velocities) lie in -0.9 to 0.9. The first radius row shifts by 768 cells and the last one by 0.
All inputs are finite; a program needn't handle non-finite values.
Results may differ from a plain program's by a relative error of at most 0.0003.
Values sent between devices are 32-bit elements; how exact they have to be, the bound alone decides.
A program may use at most 64 MiB of HBM per device.

v0:
```python
import jax
import jax.numpy as jnp
from jax import lax
from jax.sharding import PartitionSpec as P

ADIABATIC = 1.4
COURANT_RADIAL = 0.09
COURANT_POLAR = 0.08
COURANT_AZIMUTH = 0.18


def padded_2(shard, sides, width, wrap):
    for axis, dim in sides:
        count, length = (lax.axis_size(axis), shard.shape[dim])
        up = [(i, (i + 1) % count) for i in range(count if wrap else count - 1)]
        down = [(j, i) for i, j in up]
        last = lax.slice_in_dim(shard, length - width, length, axis=dim)
        initial = lax.slice_in_dim(shard, 0, width, axis=dim)
        before = lax.ppermute(last, axis, up)
        after = lax.ppermute(initial, axis, down)
        shard = jnp.concatenate([before, shard, after], axis=dim)
    return shard


def shifted(block, axis, distance):
    devices = range(lax.axis_size(axis))
    route = [((i - distance) % len(devices), i) for i in devices]
    return lax.ppermute(block, axis, route)


def cut_along(values, first_cell, finish, along):
    return lax.slice_in_dim(values, first_cell, finish, axis=along)


def edge_states(values, along):
    length = values.shape[along]
    before = cut_along(values, 0, length - 3, along)
    centre = cut_along(values, 1, length - 2, along)
    follow = cut_along(values, 2, length - 1, along)
    beyond = cut_along(values, 3, length, along)
    interface = 7.0 / 12.0 * (centre + follow) - 1.0 / 12.0 * (before + beyond)
    interface = jnp.clip(interface, jnp.minimum(centre, follow), jnp.maximum(centre, follow))
    count = length - 3
    left_edge = cut_along(interface, 0, count - 1, along)
    right_edge = cut_along(interface, 1, count, along)
    middle_cell = cut_along(values, 2, length - 2, along)
    no_slope = (right_edge - middle_cell) * (middle_cell - left_edge) <= 0.0
    left_edge = jnp.where(no_slope, middle_cell, left_edge)
    right_edge = jnp.where(no_slope, middle_cell, right_edge)
    spread = right_edge - left_edge
    middle = middle_cell - 0.5 * (left_edge + right_edge)
    new_left = jnp.where(
        spread * middle > spread * spread / 6.0, 3.0 * middle_cell - 2.0 * right_edge, left_edge
    )
    new_right = jnp.where(
        spread * middle < -spread * spread / 6.0, 3.0 * middle_cell - 2.0 * left_edge, right_edge
    )
    return (new_left, new_right)


def primitive_parts(state, normal):
    density = state[0]
    pressure = state[4]
    normal_speed = state[normal]
    squared = state[1] * state[1] + state[2] * state[2] + state[3] * state[3]
    energy = pressure / (ADIABATIC - 1.0) + 0.5 * density * squared
    sound_speed = jnp.sqrt(ADIABATIC * pressure / density)
    conserved = [density, density * state[1], density * state[2], density * state[3], energy]
    flux_list = [plain_term * normal_speed for plain_term in conserved]
    flux_list[normal] = flux_list[normal] + pressure
    flux_list[4] = flux_list[4] + pressure * normal_speed
    return (density, pressure, normal_speed, energy, sound_speed, conserved, flux_list)


def star_flux(state, parts, wave_speed, contact, normal):
    density, pressure, normal_speed, energy, sound_speed, conserved, flux_list = parts
    factor = density * (wave_speed - normal_speed) / (wave_speed - contact)
    star_energy = factor * (
        energy / density
        + (contact - normal_speed) * (contact + pressure / (density * (wave_speed - normal_speed)))
    )
    star_state = [factor, factor * state[1], factor * state[2], factor * state[3], star_energy]
    star_state[normal] = factor * contact
    return [
        flux_term + wave_speed * (star_term - plain_term)
        for flux_term, star_term, plain_term in zip(flux_list, star_state, conserved)
    ]


def riemann_flux(left_state, right_state, normal):
    left_parts = primitive_parts(left_state, normal)
    right_parts = primitive_parts(right_state, normal)
    slow_wave = jnp.minimum(left_parts[2] - left_parts[4], right_parts[2] - right_parts[4])
    fast_wave = jnp.maximum(left_parts[2] + left_parts[4], right_parts[2] + right_parts[4])
    mass_left = left_parts[0] * (left_parts[2] - slow_wave)
    mass_right = right_parts[0] * (fast_wave - right_parts[2])
    contact = (
        mass_left * left_parts[2] + mass_right * right_parts[2] + left_parts[1] - right_parts[1]
    ) / (mass_left + mass_right)
    star_left = star_flux(left_state, left_parts, slow_wave, contact, normal)
    star_right = star_flux(right_state, right_parts, fast_wave, contact, normal)
    merged = []
    for flux_left, inner_left, inner_right, flux_right in zip(
        left_parts[6], star_left, star_right, right_parts[6]
    ):
        merged.append(
            jnp.where(
                slow_wave >= 0.0,
                flux_left,
                jnp.where(
                    contact >= 0.0, inner_left, jnp.where(fast_wave > 0.0, inner_right, flux_right)
                ),
            )
        )
    return jnp.stack(merged)


def flux_difference(window, along, normal):
    left_edge, right_edge = edge_states(window, along)
    cell_total = left_edge.shape[along]
    from_left = cut_along(right_edge, 0, cell_total - 1, along)
    from_right = cut_along(left_edge, 1, cell_total, along)
    flux_all = riemann_flux(from_left, from_right, normal)
    faces = flux_all.shape[along]
    return cut_along(flux_all, 1, faces, along) - cut_along(flux_all, 0, faces - 1, along)


def tendency(window, courant_rows):
    padded = jnp.pad(window, ((0, 0), (0, 0), (3, 3), (0, 0)), mode="edge")
    radial_term = flux_difference(padded[:, :, 3:-3, 3:-3], 1, 1)
    polar_term = flux_difference(padded[:, 3:-3, :, 3:-3], 2, 2)
    azimuth_term = flux_difference(padded[:, 3:-3, 3:-3, :], 3, 3)
    return -(
        COURANT_RADIAL * radial_term
        + COURANT_POLAR * polar_term
        + courant_rows[None, :, None, None] * azimuth_term
    )


def courant_profile(row_index, total_rows):
    return COURANT_AZIMUTH / (1.0 + (row_index + 0.5) / total_rows)


def to_conserved(primitive):
    density = primitive[0]
    squared = (
        primitive[1] * primitive[1] + primitive[2] * primitive[2] + primitive[3] * primitive[3]
    )
    energy = primitive[4] / (ADIABATIC - 1.0) + 0.5 * density * squared
    return jnp.stack(
        [density, density * primitive[1], density * primitive[2], density * primitive[3], energy]
    )


def to_primitive(conserved):
    density = conserved[0]
    velocity = conserved[1:4] / density
    squared = velocity[0] * velocity[0] + velocity[1] * velocity[1] + velocity[2] * velocity[2]
    pressure = (ADIABATIC - 1.0) * (conserved[4] - 0.5 * density * squared)
    return jnp.concatenate([density[None], velocity, pressure[None]])


def fix_edges(extended, inner, depth):
    rad_index = lax.axis_index("rad")
    last_index = lax.axis_size("rad") - 1
    lower_rim = jnp.where(
        rad_index == 0,
        jnp.broadcast_to(inner[:, :1], extended[:, :depth].shape),
        extended[:, :depth],
    )
    upper_rim = jnp.where(
        rad_index == last_index,
        jnp.broadcast_to(inner[:, -1:], extended[:, -depth:].shape),
        extended[:, -depth:],
    )
    return jnp.concatenate([lower_rim, extended[:, depth:-depth], upper_rim], axis=1)


def extend_deep(primitive):
    widened = padded_2(primitive, (("rad", 1),), 6, False)
    widened = fix_edges(widened, primitive, 6)
    return padded_2(widened, (("az", 3),), 6, True)


def pick_rows(blocks, quotient):
    chosen = blocks[0]
    for distance in range(1, len(blocks)):
        chosen = jnp.where((quotient == distance)[None, :, None, None], blocks[distance], chosen)
    return chosen


def roll_rows(farther, current, remainder):
    joined = jnp.concatenate([farther, current], axis=3)
    cell_count = current.shape[3]

    def slice_row(one_row, amount):
        return lax.dynamic_slice_in_dim(one_row, cell_count - amount, cell_count, axis=2)

    return jax.vmap(slice_row, in_axes=(1, 0), out_axes=1)(joined, remainder)


def shift_rows(primitive, quotient, remainder):
    blocks = [primitive]
    for distance in range(1, 4):
        blocks.append(shifted(primitive, "az", distance))
    current = pick_rows(blocks, quotient)
    farther = pick_rows(blocks[1:] + [jnp.zeros_like(primitive)], quotient)
    return roll_rows(farther, current, remainder)


def on_device(fields, shifts):
    row_count = fields.shape[1]
    cell_count = fields.shape[3]
    rad_index = lax.axis_index("rad")
    total_rows = row_count * lax.axis_size("rad")
    inner_rows = (rad_index * row_count + jnp.arange(row_count, dtype=jnp.int32)).astype(
        jnp.float32
    )
    courant_inner = courant_profile(inner_rows, total_rows)
    quotient = shifts // cell_count
    remainder = shifts - quotient * cell_count
    current = fields
    outer_rows = (rad_index * row_count - 3 + jnp.arange(row_count + 6, dtype=jnp.int32)).astype(
        jnp.float32
    )
    courant_outer = courant_profile(outer_rows, total_rows)
    extended = extend_deep(current)
    initial_wide = to_conserved(extended[:, 3:-3, :, 3:-3])
    section_one_wide = initial_wide + tendency(extended, courant_outer)
    section_one_prim = to_primitive(section_one_wide)
    section_one_prim = fix_edges(section_one_prim, section_one_prim[:, 3:-3], 3)
    initial = initial_wide[:, 3:-3, :, 3:-3]
    section_one = section_one_wide[:, 3:-3, :, 3:-3]
    section_two = 0.5 * initial + 0.5 * (section_one + tendency(section_one_prim, courant_inner))
    current = shift_rows(to_primitive(section_two), quotient, remainder)
    return current


def solution(mesh):
    in_specs = (P(None, "rad", None, "az"), P("rad"))
    out_specs = P(None, "rad", None, "az")
    return jax.shard_map(
        on_device, mesh=mesh, in_specs=in_specs, out_specs=out_specs, check_vma=False
    )
```

profile of v0, /device:TPU:13, one launch (start us, length us, event | category | flops | bytes accessed | tf_op | source)
XLA Modules:
  0.0 106.1 jit_solution(226922155932850803)
XLA Ops:
  0.0 3.7 %collective-permute-start = (f32[5,6,8,256]{3,2,1,0:T(8,128)}, f32[5,6,8,256]{3,2,1,0:T(8,128)S(1)}, u32[]{:S(2)}, u32[]{:S(2)}) collective-permute-start(f32[5,6,8,256]{3,2,1,0:T(8,128)} %param.2), channel_id=1, source_target_pairs={{0,4},{4,8},{8,12},{12,16},{16,20},{20,24},{24,28},{1,5},{5,9},{9,... | collective-permute-start | bytes 737288 | tf_op jit(solution)/shard_map/ppermute | solution.py:19
  3.7 1.9 %collective-permute-start.1 = (f32[5,6,8,256]{3,2,1,0:T(8,128)}, f32[5,6,8,256]{3,2,1,0:T(8,128)S(1)}, u32[]{:S(2)}, u32[]{:S(2)}) collective-permute-start(f32[5,6,8,256]{3,2,1,0:T(8,128)} %param.2), channel_id=1, source_target_pairs={{4,0},{8,4},{12,8},{16,12},{20,16},{24,20},{28,24},{5,1},{9,5},{13... | collective-permute-start | bytes 737288 | tf_op jit(solution)/shard_map/ppermute | solution.py:20
  5.6 0.8 slice_bitcast_fusion.1
  6.4 0.7 collective-permute-done
  7.1 4.3 %collective-permute-done.1 = f32[5,6,8,256]{3,2,1,0:T(8,128)S(1)} collective-permute-done((f32[5,6,8,256]{3,2,1,0:T(8,128)}, f32[5,6,8,256]{3,2,1,0:T(8,128)S(1)}, u32[]{:S(2)}, u32[]{:S(2)}) %collective-permute-start.1) | collective-permute-done | bytes 245792 | tf_op jit(solution)/shard_map/ppermute | solution.py:20
  11.4 1.1 pad_maximum_fusion.13
  12.7 1.3 %collective-permute-start.2 = (f32[5,18,8,6]{3,2,1,0:T(8,128)S(1)}, f32[5,18,8,6]{3,2,1,0:T(8,128)S(1)}, u32[]{:S(2)}, u32[]{:S(2)}) collective-permute-start(f32[5,18,8,6]{3,2,1,0:T(8,128)S(1)} %get-tuple-element.31), channel_id=1, source_target_pairs={{0,1},{1,2},{2,3},{3,0},{4,5},{5,6},{6,7},{7,4},{8,9},{9,10},{10,1... | collective-permute-start | bytes 51848 | tf_op jit(solution)/shard_map/ppermute | solution.py:19
  14.2 8.9 %collective-permute-done.2 = f32[5,18,8,6]{3,2,1,0:T(8,128)S(1)} collective-permute-done((f32[5,18,8,6]{3,2,1,0:T(8,128)S(1)}, f32[5,18,8,6]{3,2,1,0:T(8,128)S(1)}, u32[]{:S(2)}, u32[]{:S(2)}) %collective-permute-start.2) | collective-permute-done | bytes 17312 | tf_op jit(solution)/shard_map/ppermute | solution.py:19
  23.1 8.9 %collective-permute-done.3 = f32[5,18,8,6]{3,2,1,0:T(8,128)S(1)} collective-permute-done((f32[5,18,8,6]{3,2,1,0:T(8,128)S(1)}, f32[5,18,8,6]{3,2,1,0:T(8,128)S(1)}, u32[]{:S(2)}, u32[]{:S(2)}) %collective-permute-start.3) | collective-permute-done | bytes 17312 | tf_op jit(solution)/shard_map/ppermute | solution.py:20
  32.0 0.5 pad_maximum_fusion.12
  32.7 0.6 fusion.26
  33.4 1.0 fusion.12
  35.2 0.7 subtract_select_fusion.4
  35.9 0.4 fusion.113
  36.3 0.4 fusion.116
  36.7 0.4 fusion.119
  37.1 0.4 fusion.122
  37.5 0.6 fusion.125
  38.1 0.8 subtract_select_fusion.2
  38.9 0.3 fusion.91
  39.2 0.4 fusion.94
  39.6 0.4 fusion.97
  39.9 0.4 fusion.100
  40.3 0.5 fusion.103
  41.0 1.0 pad_maximum_fusion
  42.0 4.0 %fusion.6 = f32[5,12,11,262]{3,2,1,0:T(8,128)S(1)} fusion(f32[5,18,3,268]{3,2,1,0:T(4,128)S(1)} %reshape.42, f32[5,18,8,6]{3,2,1,0:T(8,128)S(1)} %collective-permute-done.3, f32[5,18,8,6]{3,2,1,0:T(8,128)S(1)} %collective-permute-done.2, f32[5,6,8,256]{3,2,1,0:T(8,128)S(1)} %broadcast_select_fusion, f32[5,6,8,256]{3,2,1,0:T(8,128)S(1)} %copy-done, ...), kind=kLoop, calls=%fused_computation.10 | loop fusion | flops 3285480 | bytes 3425760 | tf_op jit(solution)/shard_map/jit(clip)/min | solution.py:42
  46.1 1.5 %subtract_select_fusion = (f32[5,12,10,262]{3,2,1,0:T(8,128)S(1)}, f32[5,12,10,262]{3,2,1,0:T(8,128)S(1)}) fusion(f32[5,18,14,268]{3,2,1,0:T(8,128)S(1)} %pad_maximum_fusion, f32[5,12,11,262]{3,2,1,0:T(8,128)S(1)} %fusion.6), kind=kLoop, calls=%fused_computation.21 | loop fusion | flops 3930000 | bytes 3144000 | tf_op jit(solution)/shard_map/jit(_where)/select_n | solution.py:52
  47.6 0.6 fusion.60
  48.3 0.7 fusion.63
  49.0 0.7 fusion.66
  49.7 0.7 fusion.69
  50.4 1.0 fusion.72
  51.4 0.4 fusion.22
  52.1 0.4 fusion.46
  52.8 0.4 subtract_select_fusion.8
  54.4 0.5 fusion.51
  54.9 0.3 subtract_select_fusion.10
  56.5 0.7 fusion.38
  57.1 0.5 subtract_select_fusion.6
  57.9 0.5 fusion.145
  58.9 0.4 fusion.154
  60.0 2.1 %collective-permute-start.5 = (f32[5,6,8,256]{3,2,1,0:T(8,128)S(1)}, f32[5,6,8,256]{3,2,1,0:T(8,128)S(1)}, u32[]{:S(2)}, u32[]{:S(2)}) collective-permute-start(f32[5,6,8,256]{3,2,1,0:T(8,128)S(1)} %pad_maximum_fusion.25), channel_id=1, source_target_pairs={{2,0},{3,1},{0,2},{1,3},{6,4},{7,5},{4,6},{5,7},{10,8},{11,9},{8,1... | collective-permute-start | bytes 737288 | tf_op jit(solution)/shard_map/ppermute | solution.py:28
  62.3 4.5 %collective-permute-done.6 = f32[5,6,8,256]{3,2,1,0:T(8,128)S(1)} collective-permute-done((f32[5,6,8,256]{3,2,1,0:T(8,128)S(1)}, f32[5,6,8,256]{3,2,1,0:T(8,128)S(1)}, u32[]{:S(2)}, u32[]{:S(2)}) %collective-permute-start.6) | collective-permute-done | bytes 245792 | tf_op jit(solution)/shard_map/ppermute | solution.py:28
  66.8 13.6 %collective-permute-done.5 = f32[5,6,8,256]{3,2,1,0:T(8,128)S(1)} collective-permute-done((f32[5,6,8,256]{3,2,1,0:T(8,128)S(1)}, f32[5,6,8,256]{3,2,1,0:T(8,128)S(1)}, u32[]{:S(2)}, u32[]{:S(2)}) %collective-permute-start.5) | collective-permute-done | bytes 245792 | tf_op jit(solution)/shard_map/ppermute | solution.py:28
  80.4 3.9 %collective-permute-done.4 = f32[5,6,8,256]{3,2,1,0:T(8,128)S(1)} collective-permute-done((f32[5,6,8,256]{3,2,1,0:T(8,128)S(1)}, f32[5,6,8,256]{3,2,1,0:T(8,128)S(1)}, u32[]{:S(2)}, u32[]{:S(2)}) %collective-permute-start.4) | collective-permute-done | bytes 245792 | tf_op jit(solution)/shard_map/ppermute | solution.py:28
  84.6 8.5 %copy.63 = f32[5,6,8,512]{2,0,1,3:T(8,128)} copy(f32[5,6,8,512]{3,2,1,0:T(8,128)S(1)} %pad_maximum_fusion.22) | data formatting | bytes 983040 | tf_op jit(solution)/shard_map/concatenate | solution.py:193
  93.1 8.2 %gather_fusion = f32[6,5,8,256]{2,1,3,0:T(8,128)} fusion(f32[6,5,8,512]{2,1,0,3:T(8,128)} %bitcast.30, s32[6]{0:T(128)S(1)} %get-tuple-element.5), kind=kCustom, calls=%fused_computation | custom fusion | bytes 491616 | tf_op jit(solution)/shard_map/vmap()/gather | solution.py:197
  101.4 4.7 %copy.64 = f32[5,6,8,256]{3,2,1,0:T(8,128)} copy(f32[5,6,8,256]{2,0,3,1:T(8,128)} %bitcast.31) | data formatting | bytes 491520 | tf_op jit(solution)/shard_map/vmap()/transpose | solution.py:199
  (57 shorter events, 6.3 us)
Async XLA Ops:
  0.0 7.1 %collective-permute-start = (f32[5,6,8,256]{3,2,1,0:T(8,128)}, f32[5,6,8,256]{3,2,1,0:T(8,128)S(1)}, u32[]{:S(2)}, u32[]{:S(2)}) collective-permute-start(f32[5,6,8,256]{3,2,1,0:T(8,128)} %param.2), channel_id=1, source_target_pairs={{0,4},{4,8},{8,12},{12,16},{16,20},{20,24},{24,28},{1,5},{5,9},{9,... | collective-permute-start | bytes 737288 | tf_op jit(solution)/shard_map/ppermute | solution.py:19
  3.7 7.7 %collective-permute-start.1 = (f32[5,6,8,256]{3,2,1,0:T(8,128)}, f32[5,6,8,256]{3,2,1,0:T(8,128)S(1)}, u32[]{:S(2)}, u32[]{:S(2)}) collective-permute-start(f32[5,6,8,256]{3,2,1,0:T(8,128)} %param.2), channel_id=1, source_target_pairs={{4,0},{8,4},{12,8},{16,12},{20,16},{24,20},{28,24},{5,1},{9,5},{13... | collective-permute-start | bytes 737288 | tf_op jit(solution)/shard_map/ppermute | solution.py:20
  11.4 20.6 %copy-start = (f32[5,6,8,256]{3,2,1,0:T(8,128)S(1)}, f32[5,6,8,256]{3,2,1,0:T(8,128)}, u32[]{:S(2)}) copy-start(f32[5,6,8,256]{3,2,1,0:T(8,128)} %param.2) | copy-start | bytes 737284
  12.7 10.5 %collective-permute-start.2 = (f32[5,18,8,6]{3,2,1,0:T(8,128)S(1)}, f32[5,18,8,6]{3,2,1,0:T(8,128)S(1)}, u32[]{:S(2)}, u32[]{:S(2)}) collective-permute-start(f32[5,18,8,6]{3,2,1,0:T(8,128)S(1)} %get-tuple-element.31), channel_id=1, source_target_pairs={{0,1},{1,2},{2,3},{3,0},{4,5},{5,6},{6,7},{7,4},{8,9},{9,10},{10,1... | collective-permute-start | bytes 51848 | tf_op jit(solution)/shard_map/ppermute | solution.py:19
  14.0 18.0 %collective-permute-start.3 = (f32[5,18,8,6]{3,2,1,0:T(8,128)S(1)}, f32[5,18,8,6]{3,2,1,0:T(8,128)S(1)}, u32[]{:S(2)}, u32[]{:S(2)}) collective-permute-start(f32[5,18,8,6]{3,2,1,0:T(8,128)S(1)} %get-tuple-element.32), channel_id=1, source_target_pairs={{1,0},{2,1},{3,2},{0,3},{5,4},{6,5},{7,6},{4,7},{9,8},{10,9},{11,1... | collective-permute-start | bytes 51848 | tf_op jit(solution)/shard_map/ppermute | solution.py:20
  59.3 3.0 %copy-start.1 = (s32[6]{0:T(128)S(1)}, s32[6]{0:T(128)}, u32[]{:S(2)}) copy-start(s32[6]{0:T(128)} %param.3) | copy-start | bytes 76
  59.7 7.1 %collective-permute-start.6 = (f32[5,6,8,256]{3,2,1,0:T(8,128)S(1)}, f32[5,6,8,256]{3,2,1,0:T(8,128)S(1)}, u32[]{:S(2)}, u32[]{:S(2)}) collective-permute-start(f32[5,6,8,256]{3,2,1,0:T(8,128)S(1)} %pad_maximum_fusion.25), channel_id=1, source_target_pairs={{3,0},{0,1},{1,2},{2,3},{7,4},{4,5},{5,6},{6,7},{11,8},{8,9},{9,10... | collective-permute-start | bytes 737288 | tf_op jit(solution)/shard_map/ppermute | solution.py:28
  60.0 20.4 %collective-permute-start.5 = (f32[5,6,8,256]{3,2,1,0:T(8,128)S(1)}, f32[5,6,8,256]{3,2,1,0:T(8,128)S(1)}, u32[]{:S(2)}, u32[]{:S(2)}) collective-permute-start(f32[5,6,8,256]{3,2,1,0:T(8,128)S(1)} %pad_maximum_fusion.25), channel_id=1, source_target_pairs={{2,0},{3,1},{0,2},{1,3},{6,4},{7,5},{4,6},{5,7},{10,8},{11,9},{8,1... | collective-permute-start | bytes 737288 | tf_op jit(solution)/shard_map/ppermute | solution.py:28
  62.1 22.3 %collective-permute-start.4 = (f32[5,6,8,256]{3,2,1,0:T(8,128)S(1)}, f32[5,6,8,256]{3,2,1,0:T(8,128)S(1)}, u32[]{:S(2)}, u32[]{:S(2)}) collective-permute-start(f32[5,6,8,256]{3,2,1,0:T(8,128)S(1)} %pad_maximum_fusion.25), channel_id=1, source_target_pairs={{1,0},{2,1},{3,2},{0,3},{5,4},{6,5},{7,6},{4,7},{9,8},{10,9},{11,1... | collective-permute-start | bytes 737288 | tf_op jit(solution)/shard_map/ppermute | solution.py:28
where the time goes:
time: 106 us
  waiting for transfers between devices  44.7 us (42%)
  other arithmetic  27.9 us (26%)
  local copies, waits for them, and re-layouts  23.2 us (22%)
  starting transfers between devices  9.74 us (9%)
    ppermute x3, waiting for transfers between devices, shifted(): return lax.ppermute(block, axis, route)  22 us
    ppermute x2, waiting for transfers between devices, padded_2(): after = lax.ppermute(initial, axis, down)  13.2 us
    ppermute x2, waiting for transfers between devices, padded_2(): before = lax.ppermute(last, axis, up)  9.6 us
    unnamed x27, other arithmetic  8.84 us
    concatenate x1, local copies, waits for them, and re-layouts, roll_rows(): joined = jnp.concatenate([farther, current], axis=3)  8.54 us
    gather x1, local copies, waits for them, and re-layouts, slice_row(): lax.dynamic_slice_in_dim(one_row, cell_count - amount, cell_count, axis=2)  8.24 us
    min x6, other arithmetic, edge_states(): jnp.clip(interface, jnp.minimum(centre, follow), jnp.maximum(centre, foll...  7.19 us
    ppermute x2, starting transfers between devices, padded_2(): before = lax.ppermute(last, axis, up)  5.02 us
  transfers between devices with their start and end apart: 7, of which 7 were waited for; matrix products, arithmetic and copies ran while one was open for 1% of the time, Pallas kernels for 0%

commit v1 on v0

v1 whole, which is shorter than its diff:
```python
import functools

import jax
import jax.numpy as jnp
from jax import lax
from jax.experimental import pallas as pl
from jax.experimental.pallas import tpu as pltpu
from jax.sharding import PartitionSpec as P

ADIABATIC = 1.4
COURANT_RADIAL = 0.09
COURANT_POLAR = 0.08
COURANT_AZIMUTH = 0.18
MESH = pl.DeviceIdType.MESH
LANES = 128
DEEP = 6
SLOT = 8
PER_TILE = LANES // SLOT
REACH = 3


def pack_edges(block_ref, pack_ref, side):
    comps, rows, polar, cells = block_ref.shape
    lane = lax.broadcasted_iota(jnp.int32, (polar, LANES), 1) // SLOT
    start = 0 if side == 0 else cells - LANES
    for tile in range(pack_ref.shape[1]):
        total = jnp.zeros((polar, LANES), jnp.float32)
        for slot in range(PER_TILE):
            plane = tile * PER_TILE + slot
            if plane < comps * rows:
                part = block_ref[plane // rows, plane % rows, :, start : start + LANES]
                amount = (slot * SLOT + (0 if side == 0 else SLOT)) % LANES
                if amount:
                    part = pltpu.roll(part, amount, 1)
                total = jnp.where(lane == slot, part, total)
        pack_ref[side, tile] = total


def halo_kernel(n_rad, n_az, block_ref, low_ref, up_ref, edge_ref, pack_ref, send_sem, recv_sem):
    rad, az = lax.axis_index("rad"), lax.axis_index("az")
    right, left = lax.rem(az + 1, n_az), lax.rem(az + n_az - 1, n_az)
    has = {-1: rad > 0, 1: rad < n_rad - 1}

    def when(step, work):
        if step == 0:
            work()
        else:
            pl.when(has[step])(work)

    barrier = pltpu.get_barrier_semaphore()

    def greet(step):
        def work():
            for column in (left, right) if step == 0 else (az, left, right):
                pl.semaphore_signal(
                    barrier, inc=1, device_id={"rad": rad + step, "az": column}, device_id_type=MESH
                )

        return work

    for step in (0, -1, 1):
        when(step, greet(step))
    inside = jnp.logical_and(has[-1], has[1])
    pl.semaphore_wait(barrier, jnp.where(inside, 8, 5 if n_rad > 1 else 2))

    def radial(step):
        return pltpu.make_async_remote_copy(
            src_ref=block_ref,
            dst_ref=up_ref if step < 0 else low_ref,
            send_sem=send_sem.at[0 if step < 0 else 1],
            recv_sem=recv_sem.at[0 if step < 0 else 1],
            device_id={"rad": rad + step, "az": az},
            device_id_type=MESH,
        )

    def edge(step, side):
        slot = side * 3 + 1 - step
        return pltpu.make_async_remote_copy(
            src_ref=pack_ref.at[side],
            dst_ref=edge_ref.at[slot],
            send_sem=send_sem.at[2 + slot],
            recv_sem=recv_sem.at[2 + slot],
            device_id={"rad": rad + step, "az": left if side == 0 else right},
            device_id_type=MESH,
        )

    for step in (-1, 1):
        when(step, lambda step=step: radial(step).start())
    for side in (0, 1):
        pack_edges(block_ref, pack_ref, side)
        for step in (0, -1, 1):
            when(step, lambda step=step, side=side: edge(step, side).start())
    for side in (0, 1):
        for step in (0, -1, 1):
            when(step, lambda step=step, side=side: edge(step, side).wait_send())
            when(-step, lambda step=step, side=side: edge(step, side).wait_recv())
    for step in (-1, 1):
        when(step, lambda step=step: radial(step).wait_send())
        when(-step, lambda step=step: radial(step).wait_recv())


def interface(before, centre, follow, beyond):
    value = 7.0 / 12.0 * (centre + follow) - 1.0 / 12.0 * (before + beyond)
    return jnp.clip(value, jnp.minimum(centre, follow), jnp.maximum(centre, follow))


def limited(u, left, right):
    flat = (right - u) * (u - left) <= 0.0
    spread = right - left
    middle = u - 0.5 * (left + right)
    product = spread * middle
    sixth = spread * spread * (1.0 / 6.0)
    triple = 3.0 * u
    new_left = jnp.where(flat, u, jnp.where(product > sixth, triple - 2.0 * right, left))
    new_right = jnp.where(flat, u, jnp.where(product < -sixth, triple - 2.0 * left, right))
    return new_left, new_right


def hllc(left, right, normal):
    gas_left, gas_right = ADIABATIC * left[4], ADIABATIC * right[4]
    sound_left = gas_left * lax.rsqrt(gas_left * left[0])
    sound_right = gas_right * lax.rsqrt(gas_right * right[0])
    u_left, u_right = left[normal], right[normal]
    slow = jnp.minimum(u_left - sound_left, u_right - sound_right)
    fast = jnp.maximum(u_left + sound_left, u_right + sound_right)
    mass_left = left[0] * (u_left - slow)
    mass_right = right[0] * (fast - u_right)
    contact = (mass_left * u_left + mass_right * u_right + left[4] - right[4]) / (
        mass_left + mass_right
    )
    supersonic = slow >= 0.0
    from_left = jnp.logical_or(supersonic, contact >= 0.0)
    rho, v1, v2, v3, p = [jnp.where(from_left, a, b) for a, b in zip(left, right)]
    speeds = (None, v1, v2, v3)
    u = speeds[normal]
    wave = jnp.where(from_left, slow, fast)
    star = jnp.logical_and(slow < 0.0, jnp.logical_or(from_left, fast > 0.0))
    energy = p * (1.0 / (ADIABATIC - 1.0)) + 0.5 * rho * (v1 * v1 + v2 * v2 + v3 * v3)
    momentum = rho * u
    relative = wave - u
    mass = rho * relative
    inverse = 1.0 / (wave - contact)
    factor = mass * inverse
    star_energy = inverse * (relative * energy + (contact - u) * (mass * contact + p))
    flux_mass = momentum + jnp.where(star, wave * (factor - rho), 0.0)
    flux_normal = momentum * u + p + jnp.where(star, wave * (factor * contact - momentum), 0.0)
    flux_energy = (energy + p) * u + jnp.where(star, wave * (star_energy - energy), 0.0)
    out = [flux_mass, None, None, None, flux_energy]
    for axis in (1, 2, 3):
        out[axis] = flux_normal if axis == normal else speeds[axis] * flux_mass
    return out


def conserved_of(w):
    energy = w[4] * (1.0 / (ADIABATIC - 1.0)) + 0.5 * w[0] * (
        w[1] * w[1] + w[2] * w[2] + w[3] * w[3]
    )
    return [w[0], w[0] * w[1], w[0] * w[2], w[0] * w[3], energy]


def primitive_of(u):
    inverse = 1.0 / u[0]
    v = [inverse * u[k] for k in (1, 2, 3)]
    squared = v[0] * v[0] + v[1] * v[1] + v[2] * v[2]
    return [u[0]] + v + [(ADIABATIC - 1.0) * (u[4] - 0.5 * u[0] * squared)]


def rolled(x, amount, axis):
    return pltpu.roll(x, amount % x.shape[axis], axis)


def azimuth_difference(w):
    lows, highs = [], []
    for u in w:
        edge = interface(rolled(u, 1, 1), u, rolled(u, -1, 1), rolled(u, -2, 1))
        low, high = limited(u, rolled(edge, 1, 1), edge)
        lows.append(low)
        highs.append(rolled(high, 1, 1))
    flux = hllc(highs, lows, 3)
    return [rolled(f, -1, 1) - f for f in flux]


def polar_difference(w):
    count = w[0].shape[0]
    place = lax.broadcasted_iota(jnp.int32, w[0].shape, 0)
    first, last = place == 0, place == count - 1
    beyond_last = place >= count - 2
    lows, highs = [], []
    for u in w:
        before = jnp.where(first, u, rolled(u, 1, 0))
        follow = jnp.where(last, u, rolled(u, -1, 0))
        beyond = jnp.where(beyond_last, jnp.where(last, u, follow), rolled(u, -2, 0))
        edge = interface(before, u, follow, beyond)
        low, high = limited(u, jnp.where(first, u, rolled(edge, 1, 0)), edge)
        lows.append(low)
        highs.append(jnp.where(first, u, rolled(high, 1, 0)))
    flux = hllc(highs, lows, 2)
    rho, v1, v2, v3, p = w
    momentum = rho * v2
    energy = conserved_of(w)[4]
    outer = [momentum, momentum * v1, momentum * v2 + p, momentum * v3, (energy + p) * v2]
    return [jnp.where(last, o, rolled(f, -1, 0)) - f for f, o in zip(flux, outer)]


def row_of(ref, row, width):
    return [ref[c, row, :, :width] for c in range(5)]


def radial_start(src, cell, width, keep):
    w = [row_of(src, cell + k, width) for k in (-2, -1, 0, 1, 2)]
    for c in range(5):
        below = interface(*(w[k][c] for k in (0, 1, 2, 3)))
        above = interface(*(w[k][c] for k in (1, 2, 3, 4)))
        keep[0, c, :, :width] = above
        keep[1, c, :, :width] = limited(w[2][c], below, above)[1]


def radial_face(src, cell, width, keep):
    w = [row_of(src, cell + k, width) for k in (0, 1, 2, 3)]
    highs, lows = [], []
    for c in range(5):
        below = keep[0, c, :, :width]
        above = interface(*(w[k][c] for k in (0, 1, 2, 3)))
        low, high = limited(w[1][c], below, above)
        highs.append(keep[1, c, :, :width])
        lows.append(low)
        keep[0, c, :, :width] = above
        keep[1, c, :, :width] = high
    return hllc(highs, lows, 1)


def stage_begin(src, cell, width, keep):
    radial_start(src, cell - 1, width, keep)
    flux = radial_face(src, cell - 1, width, keep)
    for c in range(5):
        keep[2, c, :, :width] = flux[c]


def stage_row(src, cell, width, keep, courant):
    upper = radial_face(src, cell, width, keep)
    total = []
    for c in range(5):
        total.append(COURANT_RADIAL * (upper[c] - keep[2, c, :, :width]))
        keep[2, c, :, :width] = upper[c]
    w = row_of(src, cell, width)
    for c, d in enumerate(polar_difference(w)):
        total[c] += COURANT_POLAR * d
    for c, d in enumerate(azimuth_difference(row_of(src, cell, src.shape[3]))):
        total[c] += courant * d[:, :width]
    return total


def stage_kernel(
    n_rad, block_ref, low_ref, up_ref, edge_ref, out_ref, wide_ref, first_ref, half_ref, keep1, keep2
):
    comps, rows, polar, cells = block_ref.shape
    rad = lax.axis_index("rad")
    total_rows = rows * n_rad
    lane = lax.broadcasted_iota(jnp.int32, (polar, LANES), 1)

    is_first, is_last = rad == 0, rad == n_rad - 1
    for c in range(comps):
        for r in range(rows):
            wide_ref[c, DEEP + r, :, :cells] = block_ref[c, r]
        for r in range(DEEP):
            wide_ref[c, r, :, :cells] = jnp.where(is_first, block_ref[c, 0], low_ref[c, rows - DEEP + r])
            wide_ref[c, DEEP + rows + r, :, :cells] = jnp.where(
                is_last, block_ref[c, rows - 1], up_ref[c, r]
            )

    def unpacked(which, c, r):
        plane = c * rows + r
        tile, slot = plane // PER_TILE, plane % PER_TILE
        after = rolled(edge_ref[which, tile], -slot * SLOT, 1)
        before = rolled(edge_ref[3 + which, tile], -(slot * SLOT + SLOT), 1)
        return jnp.where(lane < SLOT, after, before)

    for c in range(comps):
        own = [unpacked(1, c, r) for r in range(rows)]
        for r in range(rows):
            wide_ref[c, DEEP + r, :, cells:] = own[r]
        for r in range(DEEP):
            wide_ref[c, r, :, cells:] = jnp.where(is_first, own[0], unpacked(0, c, rows - DEEP + r))
            wide_ref[c, DEEP + rows + r, :, cells:] = jnp.where(is_last, own[rows - 1], unpacked(2, c, r))

    def courant_of(row):
        index = jnp.full((1, 1), rad * rows + row, jnp.int32).astype(jnp.float32)
        return COURANT_AZIMUTH / (1.0 + (index + 0.5) / total_rows)

    width = cells + LANES
    stage_begin(wide_ref, 3, width, keep1)

    def first_row(k, carry):
        change = stage_row(wide_ref, k + 3, width, keep1, courant_of(k - 3))
        start = conserved_of(row_of(wide_ref, k + 3, width))
        new = [a - b for a, b in zip(start, change)]
        w = primitive_of(new)
        for c in range(comps):
            first_ref[c, k, :, :] = w[c]
            half_ref[c, k, :, :] = (0.5 * start[c] + 0.5 * new[c])[:, :cells]
        return carry

    lax.fori_loop(0, rows + 6, first_row, 0)

    @pl.when(is_first)
    def _():
        for r in range(3):
            first_ref[:, r] = first_ref[:, 3]

    @pl.when(is_last)
    def _():
        for r in range(3):
            first_ref[:, rows + 3 + r] = first_ref[:, rows + 2]

    stage_begin(first_ref, 3, cells, keep2)

    def second_row(i, carry):
        change = stage_row(first_ref, i + 3, cells, keep2, courant_of(i))
        w = primitive_of([half_ref[c, i + 3] - 0.5 * change[c] for c in range(comps)])
        for c in range(comps):
            out_ref[i, c] = w[c]
        return carry

    lax.fori_loop(0, rows, second_row, 0)


def turn_kernel(n_az, planes_ref, shifts_ref, out_ref, far_ref, send_sem, recv_sem):
    rad, az = lax.axis_index("rad"), lax.axis_index("az")
    rows, comps, polar, cells = planes_ref.shape
    barrier = pltpu.get_barrier_semaphore()
    for d in range(1, REACH + 1):
        for column in (lax.rem(az + d, n_az), lax.rem(az + n_az - d, n_az)):
            pl.semaphore_signal(
                barrier, inc=1, device_id={"rad": rad, "az": column}, device_id_type=MESH
            )
    pl.semaphore_wait(barrier, 2 * REACH)

    def send(d):
        return pltpu.make_async_remote_copy(
            src_ref=planes_ref,
            dst_ref=far_ref.at[d - 1],
            send_sem=send_sem.at[d - 1],
            recv_sem=recv_sem.at[d - 1],
            device_id={"rad": rad, "az": lax.rem(az + d, n_az)},
            device_id_type=MESH,
        )

    for d in range(1, REACH + 1):
        send(d).start()
    for d in range(1, REACH + 1):
        send(d).wait()
    lane = lax.broadcasted_iota(jnp.int32, (polar, cells), 1)
    for i in range(rows):
        amount = shifts_ref[i]
        quotient = amount // cells
        rest = amount - quotient * cells
        for c in range(comps):
            blocks = [planes_ref[i, c]] + [far_ref[d, i, c] for d in range(REACH)]
            near, far = blocks[0], blocks[1]
            for d in range(1, REACH + 1):
                near = jnp.where(quotient == d, blocks[d], near)
                if d < REACH:
                    far = jnp.where(quotient == d, blocks[d + 1], far)
            out_ref[c, i] = pltpu.roll(jnp.where(lane >= cells - rest, far, near), rest, 1)


def on_device(n_rad, n_az, fields, shifts):
    comps, rows, polar, cells = fields.shape
    vmem = pl.BlockSpec(memory_space=pltpu.VMEM)
    tiles = -(-comps * rows // PER_TILE)
    f32 = functools.partial(jax.ShapeDtypeStruct, dtype=jnp.float32)
    low, up, edges = pl.pallas_call(
        functools.partial(halo_kernel, n_rad, n_az),
        out_shape=(f32(fields.shape), f32(fields.shape), f32((6, tiles, polar, LANES))),
        in_specs=[vmem],
        out_specs=(vmem, vmem, vmem),
        scratch_shapes=[
            pltpu.VMEM((2, tiles, polar, LANES), jnp.float32),
            pltpu.SemaphoreType.DMA((8,)),
            pltpu.SemaphoreType.DMA((8,)),
        ],
        compiler_params=pltpu.CompilerParams(collective_id=0, has_side_effects=True),
        name="halo",
    )(fields)
    width = cells + LANES
    planes = pl.pallas_call(
        functools.partial(stage_kernel, n_rad),
        out_shape=f32((rows, comps, polar, cells)),
        in_specs=[vmem] * 4,
        out_specs=vmem,
        scratch_shapes=[
            pltpu.VMEM((comps, rows + 2 * DEEP, polar, width), jnp.float32),
            pltpu.VMEM((comps, rows + DEEP, polar, width), jnp.float32),
            pltpu.VMEM((comps, rows + DEEP, polar, cells), jnp.float32),
            pltpu.VMEM((3, comps, polar, width), jnp.float32),
            pltpu.VMEM((3, comps, polar, width), jnp.float32),
        ],
        compiler_params=pltpu.CompilerParams(vmem_limit_bytes=32 * 1024 * 1024),
        name="stages",
    )(fields, low, up, edges)
    return pl.pallas_call(
        functools.partial(turn_kernel, n_az),
        out_shape=f32(fields.shape),
        in_specs=[vmem, pl.BlockSpec(memory_space=pltpu.SMEM)],
        out_specs=vmem,
        scratch_shapes=[
            pltpu.VMEM((REACH, rows, comps, polar, cells), jnp.float32),
            pltpu.SemaphoreType.DMA((REACH,)),
            pltpu.SemaphoreType.DMA((REACH,)),
        ],
        compiler_params=pltpu.CompilerParams(collective_id=1, has_side_effects=True),
        name="turn",
    )(planes, shifts)


def solution(mesh):
    return jax.shard_map(
        functools.partial(on_device, mesh.shape["rad"], mesh.shape["az"]),
        mesh=mesh,
        in_specs=(P(None, "rad", None, "az"), P("rad")),
        out_specs=P(None, "rad", None, "az"),
        check_vma=False,
    )
```

time: 106 us -> 52.8 us (0.50)
  the two profiles are of different devices: /device:TPU:13 before, /device:TPU:11 now
where the time goes in v1:
time: 52.8 us; the launch traced here: 52.5 us
  Pallas kernels  47.5 us (90%)
  local copies, waits for them, and re-layouts  5.02 us (10%)
    pallas_call x1, Pallas kernels, on_device(): pl.pallas_call(functools.partial(turn_kernel, n_az), out_shape=f32(fields...  25.8 us
    pallas_call x1, Pallas kernels, on_device(): pl.pallas_call(functools.partial(halo_kernel, n_rad, n_az), out_shape=(f3...  12.4 us
    pallas_call x1, Pallas kernels, on_device(): pl.pallas_call(functools.partial(stage_kernel, n_rad), out_shape=f32((row...  9.19 us
    unnamed x11, local copies, waits for them, and re-layouts  5.02 us

profile of v1, /device:TPU:11, one launch (start us, length us, event | category | flops | bytes accessed | tf_op | source)
XLA Modules:
  0.0 52.5 jit_solution(284823097023503856)
XLA Ops:
  0.0 0.0 copy-start.1
  0.0 12.4 %halo.1 = (f32[5,6,8,256]{3,2,1,0:T(8,128)}, f32[5,6,8,256]{3,2,1,0:T(8,128)}, f32[6,2,8,128]{3,2,1,0:T(8,128)}) custom-call(f32[5,6,8,256]{3,2,1,0:T(8,128)} %block_ref.3), custom_call_target="tpu_custom_call" | custom-call | tf_op jit(solution)/shard_map/halo/pallas_call | solution.py:372
  12.5 0.0 copy-done.1
  12.5 0.0 copy-start.2
  12.5 0.9 %copy-done.2 = f32[5,6,8,256]{3,2,1,0:T(8,128)S(1)} copy-done((f32[5,6,8,256]{3,2,1,0:T(8,128)S(1)}, f32[5,6,8,256]{3,2,1,0:T(8,128)}, u32[]{:S(2)}) %copy-start.2) | copy-done | bytes 245784
  13.4 0.0 copy-start.3
  13.4 0.9 %copy-done.3 = f32[5,6,8,256]{3,2,1,0:T(8,128)S(1)} copy-done((f32[5,6,8,256]{3,2,1,0:T(8,128)S(1)}, f32[5,6,8,256]{3,2,1,0:T(8,128)}, u32[]{:S(2)}) %copy-start.3) | copy-done | bytes 245784
  14.4 0.0 copy-start.4
  14.4 0.8 %copy-done.4 = f32[6,2,8,128]{3,2,1,0:T(8,128)S(1)} copy-done((f32[6,2,8,128]{3,2,1,0:T(8,128)S(1)}, f32[6,2,8,128]{3,2,1,0:T(8,128)}, u32[]{:S(2)}) %copy-start.4) | copy-done | bytes 49176
  15.2 9.2 %stages.1.planes_ref = f32[6,5,8,256]{3,2,1,0:T(8,128)S(1)} custom-call(f32[5,6,8,256]{3,2,1,0:T(8,128)S(1)} %copy-done.1, f32[5,6,8,256]{3,2,1,0:T(8,128)S(1)} %copy-done.2, f32[5,6,8,256]{3,2,1,0:T(8,128)S(1)} %copy-done.3, f32[6,2,8,128]{3,2,1,0:T(8,128)S(1)} %copy-done.4), custom_call_target="tpu_custom_call" | custom-call | tf_op jit(solution)/shard_map/stages/pallas_call | solution.py:386
  24.4 0.0 copy-start
  24.4 0.7 %copy-done = f32[6,5,8,256]{3,2,1,0:T(8,128)} copy-done((f32[6,5,8,256]{3,2,1,0:T(8,128)}, f32[6,5,8,256]{3,2,1,0:T(8,128)S(1)}, u32[]{:S(2)}) %copy-start) | copy-done | bytes 245784
  25.0 25.8 %turn.1 = f32[5,6,8,256]{3,2,1,0:T(8,128)} custom-call(f32[6,5,8,256]{3,2,1,0:T(8,128)} %copy-done, s32[6]{0:T(128)} %shifts_ref.1), custom_call_target="tpu_custom_call" | custom-call | tf_op jit(solution)/shard_map/turn/pallas_call | solution.py:401
  50.9 1.7 %copy.4 = f32[5,6,8,256]{3,2,1,0:T(8,128)} copy(f32[5,6,8,256]{3,2,1,0:T(8,128)} %turn.1) | data formatting | bytes 491520
Async XLA Ops:
  0.0 12.5 %copy-start.1 = (f32[5,6,8,256]{3,2,1,0:T(8,128)S(1)}, f32[5,6,8,256]{3,2,1,0:T(8,128)}, u32[]{:S(2)}) copy-start(f32[5,6,8,256]{3,2,1,0:T(8,128)} %block_ref.3) | copy-start | bytes 737284
  12.5 0.9 %copy-start.2 = (f32[5,6,8,256]{3,2,1,0:T(8,128)S(1)}, f32[5,6,8,256]{3,2,1,0:T(8,128)}, u32[]{:S(2)}) copy-start(f32[5,6,8,256]{3,2,1,0:T(8,128)} %get-tuple-element.8.low_ref) | copy-start | bytes 737284
  13.4 0.9 %copy-start.3 = (f32[5,6,8,256]{3,2,1,0:T(8,128)S(1)}, f32[5,6,8,256]{3,2,1,0:T(8,128)}, u32[]{:S(2)}) copy-start(f32[5,6,8,256]{3,2,1,0:T(8,128)} %get-tuple-element.9.up_ref) | copy-start | bytes 737284
  14.4 0.8 %copy-start.4 = (f32[6,2,8,128]{3,2,1,0:T(8,128)S(1)}, f32[6,2,8,128]{3,2,1,0:T(8,128)}, u32[]{:S(2)}) copy-start(f32[6,2,8,128]{3,2,1,0:T(8,128)} %get-tuple-element.10.edge_ref) | copy-start | bytes 147460
  24.4 0.7 %copy-start = (f32[6,5,8,256]{3,2,1,0:T(8,128)}, f32[6,5,8,256]{3,2,1,0:T(8,128)S(1)}, u32[]{:S(2)}) copy-start(f32[6,5,8,256]{3,2,1,0:T(8,128)S(1)} %stages.1.planes_ref) | copy-start | bytes 737284

commit v2 on v1

--- a/solution.py
+++ b/solution.py
@@ -312,13 +312,15 @@
         for r in range(3):
             first_ref[:, rows + 3 + r] = first_ref[:, rows + 2]
 
+    for spare in range(rows * comps, out_ref.shape[0]):
+        out_ref[spare] = jnp.zeros((polar, cells), jnp.float32)
     stage_begin(first_ref, 3, cells, keep2)
 
     def second_row(i, carry):
         change = stage_row(first_ref, i + 3, cells, keep2, courant_of(i))
         w = primitive_of([half_ref[c, i + 3] - 0.5 * change[c] for c in range(comps)])
         for c in range(comps):
-            out_ref[i, c] = w[c]
+            out_ref[i * comps + c] = w[c]
         return carry
 
     lax.fori_loop(0, rows, second_row, 0)
@@ -326,7 +328,7 @@
 
 def turn_kernel(n_az, planes_ref, shifts_ref, out_ref, far_ref, send_sem, recv_sem):
     rad, az = lax.axis_index("rad"), lax.axis_index("az")
-    rows, comps, polar, cells = planes_ref.shape
+    comps, rows, polar, cells = out_ref.shape
     barrier = pltpu.get_barrier_semaphore()
     for d in range(1, REACH + 1):
         for column in (lax.rem(az + d, n_az), lax.rem(az + n_az - d, n_az)):
@@ -355,13 +357,86 @@
         quotient = amount // cells
         rest = amount - quotient * cells
         for c in range(comps):
-            blocks = [planes_ref[i, c]] + [far_ref[d, i, c] for d in range(REACH)]
+            blocks = [planes_ref[i * comps + c]] + [far_ref[d, i * comps + c] for d in range(REACH)]
             near, far = blocks[0], blocks[1]
             for d in range(1, REACH + 1):
                 near = jnp.where(quotient == d, blocks[d], near)
                 if d < REACH:
                     far = jnp.where(quotient == d, blocks[d + 1], far)
             out_ref[c, i] = pltpu.roll(jnp.where(lane >= cells - rest, far, near), rest, 1)
+
+
+def quarter_turn_kernel(n_az, planes_ref, shifts_ref, out_ref, far_ref, turned_ref, back_ref, send_sem, recv_sem):
+    rad, az = lax.axis_index("rad"), lax.axis_index("az")
+    comps, rows, polar, cells = out_ref.shape
+    share = planes_ref.shape[0] // n_az
+    barrier = pltpu.get_barrier_semaphore()
+    for d in range(1, n_az):
+        pl.semaphore_signal(
+            barrier, inc=1, device_id={"rad": rad, "az": lax.rem(az + d, n_az)}, device_id_type=MESH
+        )
+    pl.semaphore_wait(barrier, n_az - 1)
+
+    def gather(d):
+        owner = lax.rem(az + d, n_az)
+        return pltpu.make_async_remote_copy(
+            src_ref=planes_ref.at[pl.ds(owner * share, share)],
+            dst_ref=far_ref.at[d - 1],
+            send_sem=send_sem.at[d - 1],
+            recv_sem=recv_sem.at[d - 1],
+            device_id={"rad": rad, "az": owner},
+            device_id_type=MESH,
+        )
+
+    def home(g):
+        return pltpu.make_async_remote_copy(
+            src_ref=turned_ref.at[g],
+            dst_ref=back_ref.at[pl.ds(az * share, share)],
+            send_sem=send_sem.at[n_az - 2 + g],
+            recv_sem=recv_sem.at[n_az - 2 + g],
+            device_id={"rad": rad, "az": lax.rem(az + g, n_az)},
+            device_id_type=MESH,
+        )
+
+    for d in range(1, n_az):
+        gather(d).start()
+    for d in range(1, n_az):
+        gather(d).wait()
+    lane = lax.broadcasted_iota(jnp.int32, (polar, cells), 1)
+    for k in range(share):
+        row = jnp.minimum((az * share + k) // comps, rows - 1)
+        amount = shifts_ref[row]
+        quotient = amount // cells
+        rest = amount - quotient * cells
+        blocks = [planes_ref[az * share + k]] + [far_ref[d, k] for d in range(n_az - 1)]
+        blocks = [pltpu.roll(b, rest, 1) for b in blocks]
+        ahead = blocks
+        for q in range(1, n_az):
+            ahead = [
+                jnp.where(quotient == q, blocks[(q + j) % n_az], a) for j, a in enumerate(ahead)
+            ]
+        for g in range(n_az):
+            turned = jnp.where(lane < rest, ahead[(1 - g) % n_az], ahead[-g % n_az])
+            if g:
+                turned_ref[g, k] = turned
+            else:
+                back_ref[az * share + k] = turned
+    for g in range(1, n_az):
+        home(g).start()
+    for g in range(1, n_az):
+        home(g).wait_send()
+        sender = lax.rem(az + n_az - g, n_az)
+        pltpu.make_async_remote_copy(
+            src_ref=turned_ref.at[g],
+            dst_ref=back_ref.at[pl.ds(sender * share, share)],
+            send_sem=send_sem.at[n_az - 2 + g],
+            recv_sem=recv_sem.at[n_az - 2 + g],
+            device_id={"rad": rad, "az": lax.rem(az + g, n_az)},
+            device_id_type=MESH,
+        ).wait_recv()
+    for i in range(rows):
+        for c in range(comps):
+            out_ref[c, i] = back_ref[i * comps + c]
 
 
 def on_device(n_rad, n_az, fields, shifts):
@@ -383,9 +458,10 @@
         name="halo",
     )(fields)
     width = cells + LANES
+    count = -(-rows * comps // 8) * 8
     planes = pl.pallas_call(
         functools.partial(stage_kernel, n_rad),
-        out_shape=f32((rows, comps, polar, cells)),
+        out_shape=f32((count, polar, cells)),
         in_specs=[vmem] * 4,
         out_specs=vmem,
         scratch_shapes=[
@@ -398,13 +474,30 @@
         compiler_params=pltpu.CompilerParams(vmem_limit_bytes=32 * 1024 * 1024),
         name="stages",
     )(fields, low, up, edges)
+    if n_az == 4:
+        share = count // n_az
+        return pl.pallas_call(
+            functools.partial(quarter_turn_kernel, n_az),
+            out_shape=f32(fields.shape),
+            in_specs=[vmem, pl.BlockSpec(memory_space=pltpu.SMEM)],
+            out_specs=vmem,
+            scratch_shapes=[
+                pltpu.VMEM((n_az - 1, share, polar, cells), jnp.float32),
+                pltpu.VMEM((n_az, share, polar, cells), jnp.float32),
+                pltpu.VMEM((count, polar, cells), jnp.float32),
+                pltpu.SemaphoreType.DMA((2 * n_az - 2,)),
+                pltpu.SemaphoreType.DMA((2 * n_az - 2,)),
+            ],
+            compiler_params=pltpu.CompilerParams(collective_id=1, has_side_effects=True),
+            name="turn",
+        )(planes, shifts)
     return pl.pallas_call(
         functools.partial(turn_kernel, n_az),
         out_shape=f32(fields.shape),
         in_specs=[vmem, pl.BlockSpec(memory_space=pltpu.SMEM)],
         out_specs=vmem,
         scratch_shapes=[
-            pltpu.VMEM((REACH, rows, comps, polar, cells), jnp.float32),
+            pltpu.VMEM((REACH, count, polar, cells), jnp.float32),
             pltpu.SemaphoreType.DMA((REACH,)),
             pltpu.SemaphoreType.DMA((REACH,)),
         ],

time: 52.8 us -> 43.8 us (0.83)
  the two profiles are of different devices: /device:TPU:11 before, /device:TPU:4 now
where the time goes in v2:
time: 43.8 us; the launch traced here: 43.5 us
  Pallas kernels  38.4 us (88%)
  local copies, waits for them, and re-layouts  5.03 us (11%)
    pallas_call x1, Pallas kernels, on_device(): pl.pallas_call(functools.partial(quarter_turn_kernel, n_az), out_shape=f3...  15.2 us
    pallas_call x1, Pallas kernels, on_device(): pl.pallas_call(functools.partial(halo_kernel, n_rad, n_az), out_shape=(f3...  14 us
    pallas_call x1, Pallas kernels, on_device(): pl.pallas_call(functools.partial(stage_kernel, n_rad), out_shape=f32((cou...  9.19 us
    unnamed x11, local copies, waits for them, and re-layouts  5.03 us

profile of v2, /device:TPU:4, one launch (start us, length us, event | category | flops | bytes accessed | tf_op | source)
XLA Modules:
  0.0 43.5 jit_solution(1756175104152010598)
XLA Ops:
  0.0 0.0 copy-start.1
  0.0 14.0 %halo.1 = (f32[5,6,8,256]{3,2,1,0:T(8,128)}, f32[5,6,8,256]{3,2,1,0:T(8,128)}, f32[6,2,8,128]{3,2,1,0:T(8,128)}) custom-call(f32[5,6,8,256]{3,2,1,0:T(8,128)} %block_ref.3), custom_call_target="tpu_custom_call" | custom-call | tf_op jit(solution)/shard_map/halo/pallas_call | solution.py:447
  14.0 0.0 copy-done.1
  14.0 0.0 copy-start.2
  14.0 0.9 %copy-done.2 = f32[5,6,8,256]{3,2,1,0:T(8,128)S(1)} copy-done((f32[5,6,8,256]{3,2,1,0:T(8,128)S(1)}, f32[5,6,8,256]{3,2,1,0:T(8,128)}, u32[]{:S(2)}) %copy-start.2) | copy-done | bytes 245784
  14.9 0.0 copy-start.3
  14.9 0.9 %copy-done.3 = f32[5,6,8,256]{3,2,1,0:T(8,128)S(1)} copy-done((f32[5,6,8,256]{3,2,1,0:T(8,128)S(1)}, f32[5,6,8,256]{3,2,1,0:T(8,128)}, u32[]{:S(2)}) %copy-start.3) | copy-done | bytes 245784
  15.9 0.0 copy-start.4
  15.9 0.8 %copy-done.4 = f32[6,2,8,128]{3,2,1,0:T(8,128)S(1)} copy-done((f32[6,2,8,128]{3,2,1,0:T(8,128)S(1)}, f32[6,2,8,128]{3,2,1,0:T(8,128)}, u32[]{:S(2)}) %copy-start.4) | copy-done | bytes 49176
  16.7 9.2 %stages.1.planes_ref = f32[32,8,256]{2,1,0:T(8,128)S(1)} custom-call(f32[5,6,8,256]{3,2,1,0:T(8,128)S(1)} %copy-done.1, f32[5,6,8,256]{3,2,1,0:T(8,128)S(1)} %copy-done.2, f32[5,6,8,256]{3,2,1,0:T(8,128)S(1)} %copy-done.3, f32[6,2,8,128]{3,2,1,0:T(8,128)S(1)} %copy-done.4), custom_call_target="tpu_custom_call" | custom-call | tf_op jit(solution)/shard_map/stages/pallas_call | solution.py:462
  25.9 0.0 copy-start
  25.9 0.7 %copy-done = f32[32,8,256]{2,1,0:T(8,128)} copy-done((f32[32,8,256]{2,1,0:T(8,128)}, f32[32,8,256]{2,1,0:T(8,128)S(1)}, u32[]{:S(2)}) %copy-start) | copy-done | bytes 262168
  26.6 15.2 %turn.1 = f32[5,6,8,256]{3,2,1,0:T(8,128)} custom-call(f32[32,8,256]{2,1,0:T(8,128)} %copy-done, s32[6]{0:T(128)} %shifts_ref.1), custom_call_target="tpu_custom_call" | custom-call | tf_op jit(solution)/shard_map/turn/pallas_call | solution.py:479
  41.8 1.7 %copy.4 = f32[5,6,8,256]{3,2,1,0:T(8,128)} copy(f32[5,6,8,256]{3,2,1,0:T(8,128)} %turn.1) | data formatting | bytes 491520
Async XLA Ops:
  0.0 14.0 %copy-start.1 = (f32[5,6,8,256]{3,2,1,0:T(8,128)S(1)}, f32[5,6,8,256]{3,2,1,0:T(8,128)}, u32[]{:S(2)}) copy-start(f32[5,6,8,256]{3,2,1,0:T(8,128)} %block_ref.3) | copy-start | bytes 737284
  14.0 0.9 %copy-start.2 = (f32[5,6,8,256]{3,2,1,0:T(8,128)S(1)}, f32[5,6,8,256]{3,2,1,0:T(8,128)}, u32[]{:S(2)}) copy-start(f32[5,6,8,256]{3,2,1,0:T(8,128)} %get-tuple-element.8.low_ref) | copy-start | bytes 737284
  14.9 0.9 %copy-start.3 = (f32[5,6,8,256]{3,2,1,0:T(8,128)S(1)}, f32[5,6,8,256]{3,2,1,0:T(8,128)}, u32[]{:S(2)}) copy-start(f32[5,6,8,256]{3,2,1,0:T(8,128)} %get-tuple-element.9.up_ref) | copy-start | bytes 737284
  15.9 0.8 %copy-start.4 = (f32[6,2,8,128]{3,2,1,0:T(8,128)S(1)}, f32[6,2,8,128]{3,2,1,0:T(8,128)}, u32[]{:S(2)}) copy-start(f32[6,2,8,128]{3,2,1,0:T(8,128)} %get-tuple-element.10.edge_ref) | copy-start | bytes 147460
  25.9 0.7 %copy-start = (f32[32,8,256]{2,1,0:T(8,128)}, f32[32,8,256]{2,1,0:T(8,128)S(1)}, u32[]{:S(2)}) copy-start(f32[32,8,256]{2,1,0:T(8,128)S(1)} %stages.1.planes_ref) | copy-start | bytes 786436

commit v3 on v2

--- a/solution.py
+++ b/solution.py
@@ -366,7 +366,7 @@
             out_ref[c, i] = pltpu.roll(jnp.where(lane >= cells - rest, far, near), rest, 1)
 
 
-def quarter_turn_kernel(n_az, planes_ref, shifts_ref, out_ref, far_ref, turned_ref, back_ref, send_sem, recv_sem):
+def quarter_turn_kernel(n_rad, n_az, block_ref, low_ref, up_ref, edge_ref, shifts_ref, out_ref, far_ref, turned_ref, back_ref, send_sem, recv_sem, planes_ref, *stage_refs):
     rad, az = lax.axis_index("rad"), lax.axis_index("az")
     comps, rows, polar, cells = out_ref.shape
     share = planes_ref.shape[0] // n_az
@@ -375,6 +375,7 @@
         pl.semaphore_signal(
             barrier, inc=1, device_id={"rad": rad, "az": lax.rem(az + d, n_az)}, device_id_type=MESH
         )
+    stage_kernel(n_rad, block_ref, low_ref, up_ref, edge_ref, planes_ref, *stage_refs)
     pl.semaphore_wait(barrier, n_az - 1)
 
     def gather(d):
@@ -459,27 +460,19 @@
     )(fields)
     width = cells + LANES
     count = -(-rows * comps // 8) * 8
-    planes = pl.pallas_call(
-        functools.partial(stage_kernel, n_rad),
-        out_shape=f32((count, polar, cells)),
-        in_specs=[vmem] * 4,
-        out_specs=vmem,
-        scratch_shapes=[
-            pltpu.VMEM((comps, rows + 2 * DEEP, polar, width), jnp.float32),
-            pltpu.VMEM((comps, rows + DEEP, polar, width), jnp.float32),
-            pltpu.VMEM((comps, rows + DEEP, polar, cells), jnp.float32),
-            pltpu.VMEM((3, comps, polar, width), jnp.float32),
-            pltpu.VMEM((3, comps, polar, width), jnp.float32),
-        ],
-        compiler_params=pltpu.CompilerParams(vmem_limit_bytes=32 * 1024 * 1024),
-        name="stages",
-    )(fields, low, up, edges)
+    stage_scratch = [
+        pltpu.VMEM((comps, rows + 2 * DEEP, polar, width), jnp.float32),
+        pltpu.VMEM((comps, rows + DEEP, polar, width), jnp.float32),
+        pltpu.VMEM((comps, rows + DEEP, polar, cells), jnp.float32),
+        pltpu.VMEM((3, comps, polar, width), jnp.float32),
+        pltpu.VMEM((3, comps, polar, width), jnp.float32),
+    ]
     if n_az == 4:
         share = count // n_az
         return pl.pallas_call(
-            functools.partial(quarter_turn_kernel, n_az),
+            functools.partial(quarter_turn_kernel, n_rad, n_az),
             out_shape=f32(fields.shape),
-            in_specs=[vmem, pl.BlockSpec(memory_space=pltpu.SMEM)],
+            in_specs=[vmem] * 4 + [pl.BlockSpec(memory_space=pltpu.SMEM)],
             out_specs=vmem,
             scratch_shapes=[
                 pltpu.VMEM((n_az - 1, share, polar, cells), jnp.float32),
@@ -487,10 +480,23 @@
                 pltpu.VMEM((count, polar, cells), jnp.float32),
                 pltpu.SemaphoreType.DMA((2 * n_az - 2,)),
                 pltpu.SemaphoreType.DMA((2 * n_az - 2,)),
+                pltpu.VMEM((count, polar, cells), jnp.float32),
+                *stage_scratch,
             ],
-            compiler_params=pltpu.CompilerParams(collective_id=1, has_side_effects=True),
-            name="turn",
-        )(planes, shifts)
+            compiler_params=pltpu.CompilerParams(
+                collective_id=1, has_side_effects=True, vmem_limit_bytes=32 * 1024 * 1024
+            ),
+            name="stages_turn",
+        )(fields, low, up, edges, shifts)
+    planes = pl.pallas_call(
+        functools.partial(stage_kernel, n_rad),
+        out_shape=f32((count, polar, cells)),
+        in_specs=[vmem] * 4,
+        out_specs=vmem,
+        scratch_shapes=stage_scratch,
+        compiler_params=pltpu.CompilerParams(vmem_limit_bytes=32 * 1024 * 1024),
+        name="stages",
+    )(fields, low, up, edges)
     return pl.pallas_call(
         functools.partial(turn_kernel, n_az),
         out_shape=f32(fields.shape),

time: 43.8 us -> 39.5 us (0.902)
  the two profiles are of different devices: /device:TPU:4 before, /device:TPU:27 now
where the time goes in v3:
time: 39.5 us; the launch traced here: 39.3 us
  Pallas kernels  35.2 us (89%)
  local copies, waits for them, and re-layouts  4.03 us (10%)
    pallas_call x1, Pallas kernels, on_device(): pl.pallas_call(functools.partial(quarter_turn_kernel, n_rad, n_az), out_s...  23.8 us
    pallas_call x1, Pallas kernels, on_device(): pl.pallas_call(functools.partial(halo_kernel, n_rad, n_az), out_shape=(f3...  11.4 us
    unnamed x11, local copies, waits for them, and re-layouts  4.03 us

profile of v3, /device:TPU:27, one launch (start us, length us, event | category | flops | bytes accessed | tf_op | source)
XLA Modules:
  0.0 39.3 jit_solution(15907590342767649893)
XLA Ops:
  0.0 0.0 copy-start
  0.0 11.4 %halo.1 = (f32[5,6,8,256]{3,2,1,0:T(8,128)}, f32[5,6,8,256]{3,2,1,0:T(8,128)}, f32[6,2,8,128]{3,2,1,0:T(8,128)}) custom-call(f32[5,6,8,256]{3,2,1,0:T(8,128)} %block_ref.3), custom_call_target="tpu_custom_call" | custom-call | tf_op jit(solution)/shard_map/halo/pallas_call | solution.py:448
  11.4 0.0 copy-start.4
  11.5 0.0 copy-done
  11.5 0.6 %copy-done.4 = s32[6]{0:T(128)S(1)} copy-done((s32[6]{0:T(128)S(1)}, s32[6]{0:T(128)}, u32[]{:S(2)}) %copy-start.4) | copy-done | bytes 48
  12.1 0.0 copy-start.1
  12.1 0.9 %copy-done.1 = f32[5,6,8,256]{3,2,1,0:T(8,128)S(1)} copy-done((f32[5,6,8,256]{3,2,1,0:T(8,128)S(1)}, f32[5,6,8,256]{3,2,1,0:T(8,128)}, u32[]{:S(2)}) %copy-start.1) | copy-done | bytes 245784
  13.0 0.0 copy-start.2
  13.0 0.9 %copy-done.2 = f32[5,6,8,256]{3,2,1,0:T(8,128)S(1)} copy-done((f32[5,6,8,256]{3,2,1,0:T(8,128)S(1)}, f32[5,6,8,256]{3,2,1,0:T(8,128)}, u32[]{:S(2)}) %copy-start.2) | copy-done | bytes 245784
  14.0 0.0 copy-start.3
  14.0 0.8 %copy-done.3 = f32[6,2,8,128]{3,2,1,0:T(8,128)S(1)} copy-done((f32[6,2,8,128]{3,2,1,0:T(8,128)S(1)}, f32[6,2,8,128]{3,2,1,0:T(8,128)}, u32[]{:S(2)}) %copy-start.3) | copy-done | bytes 49176
  14.8 23.8 %stages_turn.1 = f32[5,6,8,256]{3,2,1,0:T(8,128)S(1)} custom-call(f32[5,6,8,256]{3,2,1,0:T(8,128)S(1)} %copy-done, f32[5,6,8,256]{3,2,1,0:T(8,128)S(1)} %copy-done.1, f32[5,6,8,256]{3,2,1,0:T(8,128)S(1)} %copy-done.2, f32[6,2,8,128]{3,2,1,0:T(8,128)S(1)} %copy-done.3, s32[6]{0:T(128)S(1)} %copy-done.4), custom_call_target="tpu_custom_call" | custom-call | tf_op jit(solution)/shard_map/stages_turn/pallas_call | solution.py:472
  38.6 0.7 %copy.4 = f32[5,6,8,256]{3,2,1,0:T(8,128)} copy(f32[5,6,8,256]{3,2,1,0:T(8,128)S(1)} %stages_turn.1) | data formatting | bytes 491520
Async XLA Ops:
  0.0 11.5 %copy-start = (f32[5,6,8,256]{3,2,1,0:T(8,128)S(1)}, f32[5,6,8,256]{3,2,1,0:T(8,128)}, u32[]{:S(2)}) copy-start(f32[5,6,8,256]{3,2,1,0:T(8,128)} %block_ref.3) | copy-start | bytes 737284
  11.4 0.7 %copy-start.4 = (s32[6]{0:T(128)S(1)}, s32[6]{0:T(128)}, u32[]{:S(2)}) copy-start(s32[6]{0:T(128)} %shifts_ref.1) | copy-start | bytes 76
  12.1 0.9 %copy-start.1 = (f32[5,6,8,256]{3,2,1,0:T(8,128)S(1)}, f32[5,6,8,256]{3,2,1,0:T(8,128)}, u32[]{:S(2)}) copy-start(f32[5,6,8,256]{3,2,1,0:T(8,128)} %get-tuple-element.8.low_ref) | copy-start | bytes 737284
  13.0 0.9 %copy-start.2 = (f32[5,6,8,256]{3,2,1,0:T(8,128)S(1)}, f32[5,6,8,256]{3,2,1,0:T(8,128)}, u32[]{:S(2)}) copy-start(f32[5,6,8,256]{3,2,1,0:T(8,128)} %get-tuple-element.9.up_ref) | copy-start | bytes 737284
  14.0 0.8 %copy-start.3 = (f32[6,2,8,128]{3,2,1,0:T(8,128)S(1)}, f32[6,2,8,128]{3,2,1,0:T(8,128)}, u32[]{:S(2)}) copy-start(f32[6,2,8,128]{3,2,1,0:T(8,128)} %get-tuple-element.10.edge_ref) | copy-start | bytes 147460

commit v4 on v3

--- a/solution.py
+++ b/solution.py
@@ -36,7 +36,9 @@
         pack_ref[side, tile] = total
 
 
-def halo_kernel(n_rad, n_az, block_ref, low_ref, up_ref, edge_ref, pack_ref, send_sem, recv_sem):
+def halo_kernel(
+    n_rad, n_az, block_ref, low_ref, up_ref, edge_ref, pack_ref, send_sem, recv_sem, farther=()
+):
     rad, az = lax.axis_index("rad"), lax.axis_index("az")
     right, left = lax.rem(az + 1, n_az), lax.rem(az + n_az - 1, n_az)
     has = {-1: rad > 0, 1: rad < n_rad - 1}
@@ -60,8 +62,13 @@
 
     for step in (0, -1, 1):
         when(step, greet(step))
+    for d in farther:
+        pl.semaphore_signal(
+            barrier, inc=1, device_id={"rad": rad, "az": lax.rem(az + d, n_az)}, device_id_type=MESH
+        )
     inside = jnp.logical_and(has[-1], has[1])
-    pl.semaphore_wait(barrier, jnp.where(inside, 8, 5 if n_rad > 1 else 2))
+    near = jnp.where(inside, 8, 5 if n_rad > 1 else 2)
+    pl.semaphore_wait(barrier, near + len(farther))
 
     def radial(step):
         return pltpu.make_async_remote_copy(
@@ -251,7 +258,8 @@
 
 
 def stage_kernel(
-    n_rad, block_ref, low_ref, up_ref, edge_ref, out_ref, wide_ref, first_ref, half_ref, keep1, keep2
+    n_rad, block_ref, low_ref, up_ref, edge_ref, out_ref, wide_ref, first_ref, half_ref, keep1, keep2,
+    after=None,
 ):
     comps, rows, polar, cells = block_ref.shape
     rad = lax.axis_index("rad")
@@ -321,6 +329,8 @@
         w = primitive_of([half_ref[c, i + 3] - 0.5 * change[c] for c in range(comps)])
         for c in range(comps):
             out_ref[i * comps + c] = w[c]
+        if after is not None:
+            after(i)
         return carry
 
     lax.fori_loop(0, rows, second_row, 0)
@@ -366,17 +376,17 @@
             out_ref[c, i] = pltpu.roll(jnp.where(lane >= cells - rest, far, near), rest, 1)
 
 
-def quarter_turn_kernel(n_rad, n_az, block_ref, low_ref, up_ref, edge_ref, shifts_ref, out_ref, far_ref, turned_ref, back_ref, send_sem, recv_sem, planes_ref, *stage_refs):
+def quarter_turn_kernel(
+    n_rad, n_az, block_ref, shifts_ref, out_ref, low_ref, up_ref, edge_ref, pack_ref, halo_send,
+    halo_recv, far_ref, turned_ref, back_ref, send_sem, recv_sem, planes_ref, *stage_refs
+):
     rad, az = lax.axis_index("rad"), lax.axis_index("az")
     comps, rows, polar, cells = out_ref.shape
     share = planes_ref.shape[0] // n_az
-    barrier = pltpu.get_barrier_semaphore()
-    for d in range(1, n_az):
-        pl.semaphore_signal(
-            barrier, inc=1, device_id={"rad": rad, "az": lax.rem(az + d, n_az)}, device_id_type=MESH
-        )
-    stage_kernel(n_rad, block_ref, low_ref, up_ref, edge_ref, planes_ref, *stage_refs)
-    pl.semaphore_wait(barrier, n_az - 1)
+    halo_kernel(
+        n_rad, n_az, block_ref, low_ref, up_ref, edge_ref, pack_ref, halo_send, halo_recv,
+        tuple(range(2, n_az - 1)),
+    )
 
     def gather(d):
         owner = lax.rem(az + d, n_az)
@@ -399,8 +409,25 @@
             device_id_type=MESH,
         )
 
-    for d in range(1, n_az):
-        gather(d).start()
+    def after(i):
+        for owner in range(n_az):
+            last = (min((owner + 1) * share, rows * comps) - 1) // comps
+            d = lax.rem(owner - az + n_az, n_az)
+
+            @pl.when(jnp.logical_and(i == last, az != owner))
+            def _(owner=owner, d=d):
+                pltpu.make_async_remote_copy(
+                    src_ref=planes_ref.at[pl.ds(owner * share, share)],
+                    dst_ref=far_ref.at[d - 1],
+                    send_sem=send_sem.at[d - 1],
+                    recv_sem=recv_sem.at[d - 1],
+                    device_id={"rad": rad, "az": owner},
+                    device_id_type=MESH,
+                ).start()
+
+    stage_kernel(
+        n_rad, block_ref, low_ref, up_ref, edge_ref, planes_ref, *stage_refs, after=after
+    )
     for d in range(1, n_az):
         gather(d).wait()
     lane = lax.broadcasted_iota(jnp.int32, (polar, cells), 1)
@@ -445,19 +472,6 @@
     vmem = pl.BlockSpec(memory_space=pltpu.VMEM)
     tiles = -(-comps * rows // PER_TILE)
     f32 = functools.partial(jax.ShapeDtypeStruct, dtype=jnp.float32)
-    low, up, edges = pl.pallas_call(
-        functools.partial(halo_kernel, n_rad, n_az),
-        out_shape=(f32(fields.shape), f32(fields.shape), f32((6, tiles, polar, LANES))),
-        in_specs=[vmem],
-        out_specs=(vmem, vmem, vmem),
-        scratch_shapes=[
-            pltpu.VMEM((2, tiles, polar, LANES), jnp.float32),
-            pltpu.SemaphoreType.DMA((8,)),
-            pltpu.SemaphoreType.DMA((8,)),
-        ],
-        compiler_params=pltpu.CompilerParams(collective_id=0, has_side_effects=True),
-        name="halo",
-    )(fields)
     width = cells + LANES
     count = -(-rows * comps // 8) * 8
     stage_scratch = [
@@ -472,9 +486,15 @@
         return pl.pallas_call(
             functools.partial(quarter_turn_kernel, n_rad, n_az),
             out_shape=f32(fields.shape),
-            in_specs=[vmem] * 4 + [pl.BlockSpec(memory_space=pltpu.SMEM)],
+            in_specs=[vmem, pl.BlockSpec(memory_space=pltpu.SMEM)],
             out_specs=vmem,
             scratch_shapes=[
+                pltpu.VMEM(fields.shape, jnp.float32),
+                pltpu.VMEM(fields.shape, jnp.float32),
+                pltpu.VMEM((6, tiles, polar, LANES), jnp.float32),
+                pltpu.VMEM((2, tiles, polar, LANES), jnp.float32),
+                pltpu.SemaphoreType.DMA((8,)),
+                pltpu.SemaphoreType.DMA((8,)),
                 pltpu.VMEM((n_az - 1, share, polar, cells), jnp.float32),
                 pltpu.VMEM((n_az, share, polar, cells), jnp.float32),
                 pltpu.VMEM((count, polar, cells), jnp.float32),
@@ -486,8 +506,21 @@
             compiler_params=pltpu.CompilerParams(
                 collective_id=1, has_side_effects=True, vmem_limit_bytes=32 * 1024 * 1024
             ),
-            name="stages_turn",
-        )(fields, low, up, edges, shifts)
+            name="whole_step",
+        )(fields, shifts)
+    low, up, edges = pl.pallas_call(
+        functools.partial(halo_kernel, n_rad, n_az),
+        out_shape=(f32(fields.shape), f32(fields.shape), f32((6, tiles, polar, LANES))),
+        in_specs=[vmem],
+        out_specs=(vmem, vmem, vmem),
+        scratch_shapes=[
+            pltpu.VMEM((2, tiles, polar, LANES), jnp.float32),
+            pltpu.SemaphoreType.DMA((8,)),
+            pltpu.SemaphoreType.DMA((8,)),
+        ],
+        compiler_params=pltpu.CompilerParams(collective_id=0, has_side_effects=True),
+        name="halo",
+    )(fields)
     planes = pl.pallas_call(
         functools.partial(stage_kernel, n_rad),
         out_shape=f32((count, polar, cells)),

time: 39.5 us -> 34.8 us (0.88)
  the two profiles are of different devices: /device:TPU:27 before, /device:TPU:4 now
where the time goes in v4:
time: 34.8 us; the launch traced here: 34.7 us
  Pallas kernels  32.4 us (93%)
  local copies, waits for them, and re-layouts  2.29 us (7%)
    pallas_call x1, Pallas kernels, on_device(): pl.pallas_call(functools.partial(quarter_turn_kernel, n_rad, n_az), out_s...  32.4 us
    unnamed x5, local copies, waits for them, and re-layouts  2.29 us

profile of v4, /device:TPU:4, one launch (start us, length us, event | category | flops | bytes accessed | tf_op | source)
XLA Modules:
  0.0 34.7 jit_solution(4338303806050367724)
XLA Ops:
  0.0 0.0 copy-start
  0.0 0.9 %copy-done = f32[5,6,8,256]{3,2,1,0:T(8,128)S(1)} copy-done((f32[5,6,8,256]{3,2,1,0:T(8,128)S(1)}, f32[5,6,8,256]{3,2,1,0:T(8,128)}, u32[]{:S(2)}) %copy-start) | copy-done | bytes 245784
  0.9 0.0 copy-start.1
  0.9 0.7 %copy-done.1 = s32[6]{0:T(128)S(1)} copy-done((s32[6]{0:T(128)S(1)}, s32[6]{0:T(128)}, u32[]{:S(2)}) %copy-start.1) | copy-done | bytes 48
  1.6 32.4 %whole_step.1 = f32[5,6,8,256]{3,2,1,0:T(8,128)S(1)} custom-call(f32[5,6,8,256]{3,2,1,0:T(8,128)S(1)} %copy-done, s32[6]{0:T(128)S(1)} %copy-done.1), custom_call_target="tpu_custom_call" | custom-call | tf_op jit(solution)/shard_map/whole_step/pallas_call | solution.py:486
  34.0 0.7 %copy.4 = f32[5,6,8,256]{3,2,1,0:T(8,128)} copy(f32[5,6,8,256]{3,2,1,0:T(8,128)S(1)} %whole_step.1) | data formatting | bytes 491520
Async XLA Ops:
  0.0 0.9 %copy-start = (f32[5,6,8,256]{3,2,1,0:T(8,128)S(1)}, f32[5,6,8,256]{3,2,1,0:T(8,128)}, u32[]{:S(2)}) copy-start(f32[5,6,8,256]{3,2,1,0:T(8,128)} %block_ref.1) | copy-start | bytes 737284
  0.9 0.7 %copy-start.1 = (s32[6]{0:T(128)S(1)}, s32[6]{0:T(128)}, u32[]{:S(2)}) copy-start(s32[6]{0:T(128)} %shifts_ref.1) | copy-start | bytes 76

commit v5 on v4

--- a/solution.py
+++ b/solution.py
@@ -37,7 +37,8 @@
 
 
 def halo_kernel(
-    n_rad, n_az, block_ref, low_ref, up_ref, edge_ref, pack_ref, send_sem, recv_sem, farther=()
+    n_rad, n_az, block_ref, low_ref, up_ref, edge_ref, pack_ref, send_sem, recv_sem, farther=(),
+    between=None,
 ):
     rad, az = lax.axis_index("rad"), lax.axis_index("az")
     right, left = lax.rem(az + 1, n_az), lax.rem(az + n_az - 1, n_az)
@@ -98,7 +99,12 @@
         for step in (0, -1, 1):
             when(step, lambda step=step, side=side: edge(step, side).start())
     for side in (0, 1):
-        for step in (0, -1, 1):
+        edge(0, side).wait_recv()
+    if between is not None:
+        between()
+    for side in (0, 1):
+        edge(0, side).wait_send()
+        for step in (-1, 1):
             when(step, lambda step=step, side=side: edge(step, side).wait_send())
             when(-step, lambda step=step, side=side: edge(step, side).wait_recv())
     for step in (-1, 1):
@@ -243,72 +249,91 @@
         keep[2, c, :, :width] = flux[c]
 
 
-def stage_row(src, cell, width, keep, courant):
+def cross_change(src, cell, width, courant):
+    total = [COURANT_POLAR * d for d in polar_difference(row_of(src, cell, width))]
+    for c, d in enumerate(azimuth_difference(row_of(src, cell, src.shape[3]))):
+        total[c] += courant * d[:, :width]
+    return total
+
+
+def radial_change(src, cell, width, keep):
     upper = radial_face(src, cell, width, keep)
     total = []
     for c in range(5):
         total.append(COURANT_RADIAL * (upper[c] - keep[2, c, :, :width]))
         keep[2, c, :, :width] = upper[c]
-    w = row_of(src, cell, width)
-    for c, d in enumerate(polar_difference(w)):
-        total[c] += COURANT_POLAR * d
-    for c, d in enumerate(azimuth_difference(row_of(src, cell, src.shape[3]))):
-        total[c] += courant * d[:, :width]
     return total
+
+
+def courant_of(row, rows, n_rad):
+    index = jnp.full((1, 1), lax.axis_index("rad") * rows + row, jnp.int32).astype(jnp.float32)
+    return COURANT_AZIMUTH / (1.0 + (index + 0.5) / (rows * n_rad))
+
+
+def unpacked(edge_ref, which, plane):
+    lane = lax.broadcasted_iota(jnp.int32, edge_ref.shape[2:], 1)
+    tile, slot = plane // PER_TILE, plane % PER_TILE
+    after = rolled(edge_ref[which, tile], -slot * SLOT, 1)
+    before = rolled(edge_ref[3 + which, tile], -(slot * SLOT + SLOT), 1)
+    return jnp.where(lane < SLOT, after, before)
+
+
+def own_rows(n_rad, block_ref, edge_ref, wide_ref, cross_ref):
+    comps, rows, polar, cells = block_ref.shape
+    for c in range(comps):
+        for r in range(rows):
+            wide_ref[c, DEEP + r, :, :cells] = block_ref[c, r]
+            wide_ref[c, DEEP + r, :, cells:] = unpacked(edge_ref, 1, c * rows + r)
+
+    def row(r, carry):
+        change = cross_change(wide_ref, DEEP + r, cells + LANES, courant_of(r, rows, n_rad))
+        for c in range(comps):
+            cross_ref[c, r] = change[c]
+        return carry
+
+    lax.fori_loop(0, rows, row, 0)
 
 
 def stage_kernel(
     n_rad, block_ref, low_ref, up_ref, edge_ref, out_ref, wide_ref, first_ref, half_ref, keep1, keep2,
-    after=None,
+    cross_ref, after=None, own_done=False,
 ):
     comps, rows, polar, cells = block_ref.shape
     rad = lax.axis_index("rad")
-    total_rows = rows * n_rad
-    lane = lax.broadcasted_iota(jnp.int32, (polar, LANES), 1)
+    if not own_done:
+        own_rows(n_rad, block_ref, edge_ref, wide_ref, cross_ref)
 
     is_first, is_last = rad == 0, rad == n_rad - 1
     for c in range(comps):
-        for r in range(rows):
-            wide_ref[c, DEEP + r, :, :cells] = block_ref[c, r]
+        bottom, top = wide_ref[c, DEEP, :, cells:], wide_ref[c, DEEP + rows - 1, :, cells:]
         for r in range(DEEP):
-            wide_ref[c, r, :, :cells] = jnp.where(is_first, block_ref[c, 0], low_ref[c, rows - DEEP + r])
-            wide_ref[c, DEEP + rows + r, :, :cells] = jnp.where(
-                is_last, block_ref[c, rows - 1], up_ref[c, r]
+            below, above = r, DEEP + rows + r
+            low, up = c * rows + rows - DEEP + r, c * rows + r
+            wide_ref[c, below, :, :cells] = jnp.where(
+                is_first, block_ref[c, 0], low_ref[c, rows - DEEP + r]
             )
-
-    def unpacked(which, c, r):
-        plane = c * rows + r
-        tile, slot = plane // PER_TILE, plane % PER_TILE
-        after = rolled(edge_ref[which, tile], -slot * SLOT, 1)
-        before = rolled(edge_ref[3 + which, tile], -(slot * SLOT + SLOT), 1)
-        return jnp.where(lane < SLOT, after, before)
-
-    for c in range(comps):
-        own = [unpacked(1, c, r) for r in range(rows)]
-        for r in range(rows):
-            wide_ref[c, DEEP + r, :, cells:] = own[r]
-        for r in range(DEEP):
-            wide_ref[c, r, :, cells:] = jnp.where(is_first, own[0], unpacked(0, c, rows - DEEP + r))
-            wide_ref[c, DEEP + rows + r, :, cells:] = jnp.where(is_last, own[rows - 1], unpacked(2, c, r))
-
-    def courant_of(row):
-        index = jnp.full((1, 1), rad * rows + row, jnp.int32).astype(jnp.float32)
-        return COURANT_AZIMUTH / (1.0 + (index + 0.5) / total_rows)
+            wide_ref[c, above, :, :cells] = jnp.where(is_last, block_ref[c, rows - 1], up_ref[c, r])
+            wide_ref[c, below, :, cells:] = jnp.where(is_first, bottom, unpacked(edge_ref, 0, low))
+            wide_ref[c, above, :, cells:] = jnp.where(is_last, top, unpacked(edge_ref, 2, up))
 
     width = cells + LANES
     stage_begin(wide_ref, 3, width, keep1)
 
-    def first_row(k, carry):
-        change = stage_row(wide_ref, k + 3, width, keep1, courant_of(k - 3))
+    def first_row(k, own):
+        if own:
+            cross = [cross_ref[c, k - 3] for c in range(comps)]
+        else:
+            cross = cross_change(wide_ref, k + 3, width, courant_of(k - 3, rows, n_rad))
+        radial = radial_change(wide_ref, k + 3, width, keep1)
         start = conserved_of(row_of(wide_ref, k + 3, width))
-        new = [a - b for a, b in zip(start, change)]
+        new = [a - (b + d) for a, b, d in zip(start, radial, cross)]
         w = primitive_of(new)
         for c in range(comps):
             first_ref[c, k, :, :] = w[c]
             half_ref[c, k, :, :] = (0.5 * start[c] + 0.5 * new[c])[:, :cells]
-        return carry
-
-    lax.fori_loop(0, rows + 6, first_row, 0)
+
+    for begin, end, own in ((0, 3, False), (3, rows + 3, True), (rows + 3, rows + 6, False)):
+        lax.fori_loop(begin, end, lambda k, carry, own=own: (first_row(k, own), carry)[1], 0)
 
     @pl.when(is_first)
     def _():
@@ -325,7 +350,9 @@
     stage_begin(first_ref, 3, cells, keep2)
 
     def second_row(i, carry):
-        change = stage_row(first_ref, i + 3, cells, keep2, courant_of(i))
+        radial = radial_change(first_ref, i + 3, cells, keep2)
+        cross = cross_change(first_ref, i + 3, cells, courant_of(i, rows, n_rad))
+        change = [a + b for a, b in zip(radial, cross)]
         w = primitive_of([half_ref[c, i + 3] - 0.5 * change[c] for c in range(comps)])
         for c in range(comps):
             out_ref[i * comps + c] = w[c]
@@ -386,6 +413,7 @@
     halo_kernel(
         n_rad, n_az, block_ref, low_ref, up_ref, edge_ref, pack_ref, halo_send, halo_recv,
         tuple(range(2, n_az - 1)),
+        lambda: own_rows(n_rad, block_ref, edge_ref, stage_refs[0], stage_refs[-1]),
     )
 
     def gather(d):
@@ -426,7 +454,8 @@
                 ).start()
 
     stage_kernel(
-        n_rad, block_ref, low_ref, up_ref, edge_ref, planes_ref, *stage_refs, after=after
+        n_rad, block_ref, low_ref, up_ref, edge_ref, planes_ref, *stage_refs, after=after,
+        own_done=True,
     )
     for d in range(1, n_az):
         gather(d).wait()
@@ -480,6 +509,7 @@
         pltpu.VMEM((comps, rows + DEEP, polar, cells), jnp.float32),
         pltpu.VMEM((3, comps, polar, width), jnp.float32),
         pltpu.VMEM((3, comps, polar, width), jnp.float32),
+        pltpu.VMEM((comps, rows, polar, width), jnp.float32),
     ]
     if n_az == 4:
         share = count // n_az

time: 34.8 us -> 33.8 us (0.971)
  Pallas kernels: 32.4 us -> 31.1 us
    pallas_call x1, Pallas kernels: 32.4 us -> 31.1 us  [on_device(): pl.pallas_call(functools.partial(quarter_turn_kernel, n_rad, n_az), out_s...]
where the time goes in v5:
time: 33.8 us; the launch traced here: 33.4 us
  Pallas kernels  31.1 us (92%)
  local copies, waits for them, and re-layouts  2.29 us (7%)
    pallas_call x1, Pallas kernels, on_device(): pl.pallas_call(functools.partial(quarter_turn_kernel, n_rad, n_az), out_s...  31.1 us
    unnamed x5, local copies, waits for them, and re-layouts  2.29 us

profile of v5, /device:TPU:4, one launch (start us, length us, event | category | flops | bytes accessed | tf_op | source)
XLA Modules:
  0.0 33.4 jit_solution(2018198391266786226)
XLA Ops:
  0.0 0.0 copy-start
  0.0 0.9 %copy-done = f32[5,6,8,256]{3,2,1,0:T(8,128)S(1)} copy-done((f32[5,6,8,256]{3,2,1,0:T(8,128)S(1)}, f32[5,6,8,256]{3,2,1,0:T(8,128)}, u32[]{:S(2)}) %copy-start) | copy-done | bytes 245784
  0.9 0.0 copy-start.1
  0.9 0.7 %copy-done.1 = s32[6]{0:T(128)S(1)} copy-done((s32[6]{0:T(128)S(1)}, s32[6]{0:T(128)}, u32[]{:S(2)}) %copy-start.1) | copy-done | bytes 48
  1.6 31.1 %whole_step.1 = f32[5,6,8,256]{3,2,1,0:T(8,128)S(1)} custom-call(f32[5,6,8,256]{3,2,1,0:T(8,128)S(1)} %copy-done, s32[6]{0:T(128)S(1)} %copy-done.1), custom_call_target="tpu_custom_call" | custom-call | tf_op jit(solution)/shard_map/whole_step/pallas_call | solution.py:516
  32.7 0.7 %copy.4 = f32[5,6,8,256]{3,2,1,0:T(8,128)} copy(f32[5,6,8,256]{3,2,1,0:T(8,128)S(1)} %whole_step.1) | data formatting | bytes 491520
Async XLA Ops:
  0.0 0.9 %copy-start = (f32[5,6,8,256]{3,2,1,0:T(8,128)S(1)}, f32[5,6,8,256]{3,2,1,0:T(8,128)}, u32[]{:S(2)}) copy-start(f32[5,6,8,256]{3,2,1,0:T(8,128)} %block_ref.1) | copy-start | bytes 737284
  0.9 0.7 %copy-start.1 = (s32[6]{0:T(128)S(1)}, s32[6]{0:T(128)}, u32[]{:S(2)}) copy-start(s32[6]{0:T(128)} %shifts_ref.1) | copy-start | bytes 76

commit v6 on v5

--- a/solution.py
+++ b/solution.py
@@ -319,7 +319,7 @@
     width = cells + LANES
     stage_begin(wide_ref, 3, width, keep1)
 
-    def first_row(k, own):
+    def first_row(k, own, above=False):
         if own:
             cross = [cross_ref[c, k - 3] for c in range(comps)]
         else:
@@ -329,21 +329,18 @@
         new = [a - (b + d) for a, b, d in zip(start, radial, cross)]
         w = primitive_of(new)
         for c in range(comps):
-            first_ref[c, k, :, :] = w[c]
+            first_ref[c, k, :, :] = (
+                jnp.where(is_last, first_ref[c, rows + 2], w[c]) if above else w[c]
+            )
             half_ref[c, k, :, :] = (0.5 * start[c] + 0.5 * new[c])[:, :cells]
 
-    for begin, end, own in ((0, 3, False), (3, rows + 3, True), (rows + 3, rows + 6, False)):
+    for begin, end, own in ((0, 3, False), (3, 7, True)):
         lax.fori_loop(begin, end, lambda k, carry, own=own: (first_row(k, own), carry)[1], 0)
 
     @pl.when(is_first)
     def _():
         for r in range(3):
             first_ref[:, r] = first_ref[:, 3]
-
-    @pl.when(is_last)
-    def _():
-        for r in range(3):
-            first_ref[:, rows + 3 + r] = first_ref[:, rows + 2]
 
     for spare in range(rows * comps, out_ref.shape[0]):
         out_ref[spare] = jnp.zeros((polar, cells), jnp.float32)
@@ -360,7 +357,14 @@
             after(i)
         return carry
 
-    lax.fori_loop(0, rows, second_row, 0)
+    def both(i, carry, above):
+        second_row(i, 0)
+        first_row(i + 7, not above, above)
+        return carry
+
+    lax.fori_loop(0, rows - 4, functools.partial(both, above=False), 0)
+    lax.fori_loop(rows - 4, rows - 1, functools.partial(both, above=True), 0)
+    second_row(jnp.int32(rows - 1), 0)
 
 
 def turn_kernel(n_az, planes_ref, shifts_ref, out_ref, far_ref, send_sem, recv_sem):

time: 33.8 us -> 35.5 us (1.050)
  Pallas kernels: 31.1 us -> 33.1 us
    pallas_call x1, Pallas kernels: 31.1 us -> 33.1 us  [on_device(): pl.pallas_call(functools.partial(quarter_turn_kernel, n_rad, n_az), out_s...]
where the time goes in v6:
time: 35.5 us; the launch traced here: 35.4 us
  Pallas kernels  33.1 us (93%)
  local copies, waits for them, and re-layouts  2.29 us (6%)
    pallas_call x1, Pallas kernels, on_device(): pl.pallas_call(functools.partial(quarter_turn_kernel, n_rad, n_az), out_s...  33.1 us
    unnamed x5, local copies, waits for them, and re-layouts  2.29 us

profile of v6, /device:TPU:4, one launch (start us, length us, event | category | flops | bytes accessed | tf_op | source)
XLA Modules:
  0.0 35.4 jit_solution(3080764870875964973)
XLA Ops:
  0.0 0.0 copy-start
  0.0 0.9 %copy-done = f32[5,6,8,256]{3,2,1,0:T(8,128)S(1)} copy-done((f32[5,6,8,256]{3,2,1,0:T(8,128)S(1)}, f32[5,6,8,256]{3,2,1,0:T(8,128)}, u32[]{:S(2)}) %copy-start) | copy-done | bytes 245784
  0.9 0.0 copy-start.1
  0.9 0.7 %copy-done.1 = s32[6]{0:T(128)S(1)} copy-done((s32[6]{0:T(128)S(1)}, s32[6]{0:T(128)}, u32[]{:S(2)}) %copy-start.1) | copy-done | bytes 48
  1.6 33.1 %whole_step.1 = f32[5,6,8,256]{3,2,1,0:T(8,128)S(1)} custom-call(f32[5,6,8,256]{3,2,1,0:T(8,128)S(1)} %copy-done, s32[6]{0:T(128)S(1)} %copy-done.1), custom_call_target="tpu_custom_call" | custom-call | tf_op jit(solution)/shard_map/whole_step/pallas_call | solution.py:520
  34.7 0.7 %copy.4 = f32[5,6,8,256]{3,2,1,0:T(8,128)} copy(f32[5,6,8,256]{3,2,1,0:T(8,128)S(1)} %whole_step.1) | data formatting | bytes 491520
Async XLA Ops:
  0.0 0.9 %copy-start = (f32[5,6,8,256]{3,2,1,0:T(8,128)S(1)}, f32[5,6,8,256]{3,2,1,0:T(8,128)}, u32[]{:S(2)}) copy-start(f32[5,6,8,256]{3,2,1,0:T(8,128)} %block_ref.1) | copy-start | bytes 737284
  0.9 0.7 %copy-start.1 = (s32[6]{0:T(128)S(1)}, s32[6]{0:T(128)}, u32[]{:S(2)}) copy-start(s32[6]{0:T(128)} %shifts_ref.1) | copy-start | bytes 76
